TPU v7x, 256 devices: a whole 4x4x8 slice. The times are simulated.
256 devices in a mesh: seq: 64 (over z, x, core), head: 4 (over y).
Axes of the slice: x: 4, y: 4, z: 8, core: 2. Of those that a mesh axis runs over, the one named last changes fastest.
Arguments:
- query: bfloat16 [32768, 4096], P(('seq', 'head')), may hold values from -256 to 256
- keys: bfloat16 [32768, 1024], P(('seq', 'head')), may hold values from -6 to 6
- values: bfloat16 [32768, 1024], P(('seq', 'head')), may hold values from -6 to 6
- chosen: int32 [64, 8, 3], P('seq', 'head'), may hold values from -1 to 62, as said below
Outputs:
- attended: bfloat16 [32768, 4096], P(('seq', 'head'))
Inputs may be any that keep to these rules, and one draw needn't show every extreme that they name: `chosen`: for query block b every entry is -1 or one of the blocks b - 12 to b - 1. For each head shard s, the 8 / 4 key heads s * (8 / 4) to (s + 1) * (8 / 4) - 1 together never name one block twice. Block b - 1 is named by one of them for every b >= 1; query block b names min(b, 3 * 8 / 4) blocks over those heads.
All inputs are finite; a program needn't handle non-finite values.
Results may differ from a plain program's by a relative error of at most 0.0035.
Values may be sent and summed in bfloat16 or wider, within the bound.
A program may use at most 128 MiB of HBM per device.

v0:
```python
import math

import jax
import jax.numpy as jnp
from jax import lax
from jax.sharding import PartitionSpec as P

HQ = 32
HK = 8
DH = 128
BLK = 512
TOPK = 3


def shifted(value, axis, by):
    count = lax.axis_size(axis)
    pairs = [(i, i + by) for i in range(count) if 0 <= i + by < count]
    return lax.ppermute(value, axis, pairs)


def on_device(query, keys, values, chosen):
    q_loc, k_loc, v_loc = (
        lax.all_to_all(query, "head", split_axis=1, concat_axis=0, tiled=True),
        lax.all_to_all(keys, "head", split_axis=1, concat_axis=0, tiled=True),
        lax.all_to_all(values, "head", split_axis=1, concat_axis=0, tiled=True),
    )
    nseq = lax.axis_size("seq")
    mine = lax.axis_index("seq")
    window = min(12, nseq - 1)
    hk_dev = k_loc.shape[1] // DH
    grp = HQ // HK
    scale = 1.0 / math.sqrt(DH)
    k_heads = k_loc.reshape(BLK, hk_dev, DH)
    v_heads = v_loc.reshape(BLK, hk_dev, DH)
    picks = chosen[0]
    got_key_list = []
    got_val_list = []
    marks = picks + 1
    for distance in range(1, window + 1):
        their = shifted(marks, "seq", -distance)
        head_asked = jnp.int32(0)
        for local_head in range(hk_dev):
            named = jnp.any(their[local_head] == mine + 1)
            head_asked = head_asked + jnp.where(named, local_head + 1, 0)
        head_asked = head_asked - 1
        key_send = jnp.zeros((BLK, DH), jnp.bfloat16)
        val_send = jnp.zeros((BLK, DH), jnp.bfloat16)
        for local_head in range(hk_dev):
            wanted = head_asked == local_head
            key_send = jnp.where(wanted, k_heads[:, local_head, :], key_send)
            val_send = jnp.where(wanted, v_heads[:, local_head, :], val_send)
        got_key, got_val = shifted((key_send, val_send), "seq", distance)
        got_key_list.append(got_key)
        got_val_list.append(got_val)
    got_keys = jnp.stack(got_key_list)
    got_vals = jnp.stack(got_val_list)
    lower = jnp.arange(BLK)[:, None] >= jnp.arange(BLK)[None, :]
    q_groups = q_loc.reshape(BLK, hk_dev, grp, DH)
    outputs = []
    for local_head in range(hk_dev):
        idx = picks[local_head]
        valid = idx >= 0
        safe = jnp.maximum(idx, 0)
        place = jnp.clip(mine - safe - 1, 0, window - 1)
        far_keys = got_keys[place]
        far_vals = got_vals[place]
        key_cat = jnp.concatenate(
            [k_heads[:, local_head, :], far_keys.reshape(TOPK * BLK, DH)], axis=0
        )
        val_cat = jnp.concatenate(
            [v_heads[:, local_head, :], far_vals.reshape(TOPK * BLK, DH)], axis=0
        )
        far_mask = jnp.broadcast_to(valid[None, :, None], (BLK, TOPK, BLK)).reshape(BLK, TOPK * BLK)
        mask = jnp.concatenate([lower, far_mask], axis=1)[None]
        score = (
            jnp.einsum(
                "qgd,kd->gqk", q_groups[:, local_head], key_cat, preferred_element_type=jnp.float32
            )
            * scale
        )
        score = jnp.where(mask, score, -1e30)
        top = jnp.max(score, axis=-1, keepdims=True)
        expo = jnp.where(mask, jnp.exp(score - top), 0.0)
        total = jnp.sum(expo, axis=-1, keepdims=True)
        weight = expo.astype(jnp.bfloat16)
        summed = jnp.einsum("gqk,kd->gqd", weight, val_cat, preferred_element_type=jnp.float32)
        result = (summed / total).transpose(1, 0, 2).reshape(BLK, grp * DH)
        outputs.append(result.astype(jnp.bfloat16))
    local_out = jnp.concatenate(outputs, axis=1)
    return lax.all_to_all(local_out, "head", split_axis=0, concat_axis=1, tiled=True)


def solution(mesh):
    in_specs = (
        P(("seq", "head"), None),
        P(("seq", "head"), None),
        P(("seq", "head"), None),
        P("seq", "head", None),
    )
    out_specs = P(("seq", "head"), None)
    return jax.shard_map(
        on_device, mesh=mesh, in_specs=in_specs, out_specs=out_specs, check_vma=False
    )
```

profile of v0, /device:TPU:130, one launch (start us, length us, event | category | flops | bytes accessed | tf_op | source)
XLA Modules:
  0.0 348.6 jit_solution(16304892091998158355)
XLA Ops:
  0.8 3.1 collective-permute-start.22
  3.9 2.0 collective-permute-start.20
  5.9 2.8 collective-permute-start.18
  8.7 2.3 collective-permute-start.16
  11.0 1.9 collective-permute-start.14
  14.6 4.5 %all-to-all-start = ((bf16[128,4,256]{2,0,1:T(8,128)(2,1)}), bf16[128,4,256]{2,0,1:T(8,128)(2,1)S(1)}, u32[]{:S(2)}, u32[]{:S(2)}) async-start(bf16[128,4,256]{2,0,1:T(8,128)(2,1)} %bitcast.182), calls=%async_computation | async-start | bytes 524288 | tf_op jit(solution)/shard_map/all_to_all | solution.py:24
  23.7 3.1 pad_add_fusion.1
  26.8 1.9 collective-permute-start.12
  30.7 1.9 collective-permute-start.10
  34.6 3.1 collective-permute-start.8
  39.8 3.1 collective-permute-start.6
  44.8 3.7 %collective-permute-start.4 = (s32[2,3]{1,0:T(2,128)S(1)}, s32[2,3]{1,0:T(2,128)S(1)}, u32[]{:S(2)}, u32[]{:S(2)}) collective-permute-start(s32[2,3]{1,0:T(2,128)S(1)} %add_bitcast_fusion), channel_id=1, source_target_pairs={{12,0},{16,4},{20,8},{24,12},{28,16},{32,20},{36,24},{40,28},{44,3... | collective-permute-start | bytes 80 | tf_op jit(solution)/shard_map/ppermute | solution.py:18
  50.6 2.4 collective-permute-start.2
  55.0 2.3 collective-permute-start
  65.3 4.8 %all-to-all-start.2 = ((bf16[128,4,256]{2,0,1:T(8,128)(2,1)}), bf16[128,4,256]{2,0,1:T(8,128)(2,1)S(1)}, u32[]{:S(2)}, u32[]{:S(2)}) async-start(bf16[128,4,256]{2,0,1:T(8,128)(2,1)} %bitcast.181), calls=%async_computation.2 | async-start | bytes 524288 | tf_op jit(solution)/shard_map/all_to_all | solution.py:25
  74.1 3.0 all-to-all-done.2
  77.1 3.5 %all-to-all-start.1 = ((bf16[128,4,1024]{2,0,1:T(8,128)(2,1)}), bf16[128,4,1024]{2,0,1:T(8,128)(2,1)S(1)}, u32[]{:S(2)}, u32[]{:S(2)}) async-start(bf16[128,4,1024]{2,0,1:T(8,128)(2,1)} %bitcast.180), calls=%async_computation.1 | async-start | bytes 2097152 | tf_op jit(solution)/shard_map/all_to_all | solution.py:23
  81.1 5.1 %collective-permute-start.35 = (bf16[512,128]{1,0:T(8,128)(2,1)S(1)}, bf16[512,128]{1,0:T(8,128)(2,1)S(1)}, u32[]{:S(2)}, u32[]{:S(2)}) collective-permute-start(bf16[512,128]{1,0:T(8,128)(2,1)S(1)} %get-tuple-element.29), channel_id=1, source_target_pairs={{0,48},{4,52},{8,56},{12,60},{16,64},{20,68},{24,72},{28,76},{32,8... | collective-permute-start | bytes 393224 | tf_op jit(solution)/shard_map/ppermute | solution.py:18
  87.4 7.1 %collective-permute-start.23 = (bf16[512,128]{1,0:T(8,128)(2,1)}, bf16[512,128]{1,0:T(8,128)(2,1)S(1)}, u32[]{:S(2)}, u32[]{:S(2)}) collective-permute-start(bf16[512,128]{1,0:T(8,128)(2,1)} %get-tuple-element.32), channel_id=1, source_target_pairs={{0,48},{4,52},{8,56},{12,60},{16,64},{20,68},{24,72},{28,76},{32,8... | collective-permute-start | bytes 393224 | tf_op jit(solution)/shard_map/ppermute | solution.py:18
  94.5 1.9 collective-permute-start.5
  96.4 3.6 %collective-permute-start.3 = (bf16[512,128]{1,0:T(8,128)(2,1)S(1)}, bf16[512,128]{1,0:T(8,128)(2,1)S(1)}, u32[]{:S(2)}, u32[]{:S(2)}) collective-permute-start(bf16[512,128]{1,0:T(8,128)(2,1)S(1)} %get-tuple-element.61), channel_id=1, source_target_pairs={{0,8},{4,12},{8,16},{12,20},{16,24},{20,28},{24,32},{28,36},{32,40... | collective-permute-start | bytes 393224 | tf_op jit(solution)/shard_map/ppermute | solution.py:18
  100.1 1.9 collective-permute-start.24
  102.2 4.5 %collective-permute-done.24 = bf16[512,128]{1,0:T(8,128)(2,1)S(1)} collective-permute-done((bf16[512,128]{1,0:T(8,128)(2,1)S(1)}, bf16[512,128]{1,0:T(8,128)(2,1)S(1)}, u32[]{:S(2)}, u32[]{:S(2)}) %collective-permute-start.24) | collective-permute-done | bytes 131104 | tf_op jit(solution)/shard_map/ppermute | solution.py:18
  106.7 1.9 collective-permute-start.1
  109.3 3.7 %collective-permute-done.1 = bf16[512,128]{1,0:T(8,128)(2,1)S(1)} collective-permute-done((bf16[512,128]{1,0:T(8,128)(2,1)S(1)}, bf16[512,128]{1,0:T(8,128)(2,1)S(1)}, u32[]{:S(2)}, u32[]{:S(2)}) %collective-permute-start.1) | collective-permute-done | bytes 131104 | tf_op jit(solution)/shard_map/ppermute | solution.py:18
  113.0 3.4 collective-permute-start.25
  117.0 8.9 %collective-permute-done.25 = bf16[512,128]{1,0:T(8,128)(2,1)S(1)} collective-permute-done((bf16[512,128]{1,0:T(8,128)(2,1)S(1)}, bf16[512,128]{1,0:T(8,128)(2,1)S(1)}, u32[]{:S(2)}, u32[]{:S(2)}) %collective-permute-start.25) | collective-permute-done | bytes 131104 | tf_op jit(solution)/shard_map/ppermute | solution.py:18
  125.9 1.9 collective-permute-start.26
  128.5 7.4 %collective-permute-done.26 = bf16[512,128]{1,0:T(8,128)(2,1)S(1)} collective-permute-done((bf16[512,128]{1,0:T(8,128)(2,1)S(1)}, bf16[512,128]{1,0:T(8,128)(2,1)S(1)}, u32[]{:S(2)}, u32[]{:S(2)}) %collective-permute-start.26) | collective-permute-done | bytes 131104 | tf_op jit(solution)/shard_map/ppermute | solution.py:18
  135.9 1.9 collective-permute-start.27
  138.5 8.4 %collective-permute-done.27 = bf16[512,128]{1,0:T(8,128)(2,1)S(1)} collective-permute-done((bf16[512,128]{1,0:T(8,128)(2,1)S(1)}, bf16[512,128]{1,0:T(8,128)(2,1)S(1)}, u32[]{:S(2)}, u32[]{:S(2)}) %collective-permute-start.27) | collective-permute-done | bytes 131104 | tf_op jit(solution)/shard_map/ppermute | solution.py:18
  146.9 1.9 collective-permute-start.28
  149.5 6.1 %collective-permute-done.28 = bf16[512,128]{1,0:T(8,128)(2,1)S(1)} collective-permute-done((bf16[512,128]{1,0:T(8,128)(2,1)S(1)}, bf16[512,128]{1,0:T(8,128)(2,1)S(1)}, u32[]{:S(2)}, u32[]{:S(2)}) %collective-permute-start.28) | collective-permute-done | bytes 131104 | tf_op jit(solution)/shard_map/ppermute | solution.py:18
  155.6 1.9 collective-permute-start.29
  158.2 7.8 %collective-permute-done.29 = bf16[512,128]{1,0:T(8,128)(2,1)S(1)} collective-permute-done((bf16[512,128]{1,0:T(8,128)(2,1)S(1)}, bf16[512,128]{1,0:T(8,128)(2,1)S(1)}, u32[]{:S(2)}, u32[]{:S(2)}) %collective-permute-start.29) | collective-permute-done | bytes 131104 | tf_op jit(solution)/shard_map/ppermute | solution.py:18
  166.0 1.9 collective-permute-start.30
  168.5 4.9 %collective-permute-done.30 = bf16[512,128]{1,0:T(8,128)(2,1)S(1)} collective-permute-done((bf16[512,128]{1,0:T(8,128)(2,1)S(1)}, bf16[512,128]{1,0:T(8,128)(2,1)S(1)}, u32[]{:S(2)}, u32[]{:S(2)}) %collective-permute-start.30) | collective-permute-done | bytes 131104 | tf_op jit(solution)/shard_map/ppermute | solution.py:18
  173.4 1.9 collective-permute-start.31
  176.0 6.8 %collective-permute-done.31 = bf16[512,128]{1,0:T(8,128)(2,1)S(1)} collective-permute-done((bf16[512,128]{1,0:T(8,128)(2,1)S(1)}, bf16[512,128]{1,0:T(8,128)(2,1)S(1)}, u32[]{:S(2)}, u32[]{:S(2)}) %collective-permute-start.31) | collective-permute-done | bytes 131104 | tf_op jit(solution)/shard_map/ppermute | solution.py:18
  182.9 1.9 collective-permute-start.32
  185.4 5.8 %collective-permute-done.32 = bf16[512,128]{1,0:T(8,128)(2,1)S(1)} collective-permute-done((bf16[512,128]{1,0:T(8,128)(2,1)S(1)}, bf16[512,128]{1,0:T(8,128)(2,1)S(1)}, u32[]{:S(2)}, u32[]{:S(2)}) %collective-permute-start.32) | collective-permute-done | bytes 131104 | tf_op jit(solution)/shard_map/ppermute | solution.py:18
  191.2 1.9 collective-permute-start.33
  193.8 6.4 %collective-permute-done.33 = bf16[512,128]{1,0:T(8,128)(2,1)S(1)} collective-permute-done((bf16[512,128]{1,0:T(8,128)(2,1)S(1)}, bf16[512,128]{1,0:T(8,128)(2,1)S(1)}, u32[]{:S(2)}, u32[]{:S(2)}) %collective-permute-start.33) | collective-permute-done | bytes 131104 | tf_op jit(solution)/shard_map/ppermute | solution.py:18
  200.2 1.9 collective-permute-start.34
  202.8 10.1 %collective-permute-done.34 = bf16[512,128]{1,0:T(8,128)(2,1)S(1)} collective-permute-done((bf16[512,128]{1,0:T(8,128)(2,1)S(1)}, bf16[512,128]{1,0:T(8,128)(2,1)S(1)}, u32[]{:S(2)}, u32[]{:S(2)}) %collective-permute-start.34) | collective-permute-done | bytes 131104 | tf_op jit(solution)/shard_map/ppermute | solution.py:18
  212.9 1.9 collective-permute-start.21
  215.5 1.9 collective-permute-start.19
  218.0 1.9 collective-permute-start.17
  220.6 3.4 collective-permute-start.7
  224.7 14.0 %collective-permute-done.7 = bf16[512,128]{1,0:T(8,128)(2,1)S(1)} collective-permute-done((bf16[512,128]{1,0:T(8,128)(2,1)S(1)}, bf16[512,128]{1,0:T(8,128)(2,1)S(1)}, u32[]{:S(2)}, u32[]{:S(2)}) %collective-permute-start.7) | collective-permute-done | bytes 131104 | tf_op jit(solution)/shard_map/ppermute | solution.py:18
  241.3 5.8 %collective-permute-done.9 = bf16[512,128]{1,0:T(8,128)(2,1)S(1)} collective-permute-done((bf16[512,128]{1,0:T(8,128)(2,1)S(1)}, bf16[512,128]{1,0:T(8,128)(2,1)S(1)}, u32[]{:S(2)}, u32[]{:S(2)}) %collective-permute-start.9) | collective-permute-done | bytes 131104 | tf_op jit(solution)/shard_map/ppermute | solution.py:18
  249.7 7.3 %collective-permute-done.11 = bf16[512,128]{1,0:T(8,128)(2,1)S(1)} collective-permute-done((bf16[512,128]{1,0:T(8,128)(2,1)S(1)}, bf16[512,128]{1,0:T(8,128)(2,1)S(1)}, u32[]{:S(2)}, u32[]{:S(2)}) %collective-permute-start.11) | collective-permute-done | bytes 131104 | tf_op jit(solution)/shard_map/ppermute | solution.py:18
  259.5 4.9 %collective-permute-done.13 = bf16[512,128]{1,0:T(8,128)(2,1)S(1)} collective-permute-done((bf16[512,128]{1,0:T(8,128)(2,1)S(1)}, bf16[512,128]{1,0:T(8,128)(2,1)S(1)}, u32[]{:S(2)}, u32[]{:S(2)}) %collective-permute-start.13) | collective-permute-done | bytes 131104 | tf_op jit(solution)/shard_map/ppermute | solution.py:18
  264.4 2.2 collective-permute-start.15
  267.3 6.3 %collective-permute-done.15 = bf16[512,128]{1,0:T(8,128)(2,1)S(1)} collective-permute-done((bf16[512,128]{1,0:T(8,128)(2,1)S(1)}, bf16[512,128]{1,0:T(8,128)(2,1)S(1)}, u32[]{:S(2)}, u32[]{:S(2)}) %collective-permute-start.15) | collective-permute-done | bytes 131104 | tf_op jit(solution)/shard_map/ppermute | solution.py:18
  275.0 2.0 gather_fusion.3
  277.0 2.8 gather_fusion.1
  282.7 2.8 gather_fusion.2
  285.4 2.8 gather_fusion
  290.2 11.3 %fusion.62 = (f32[4,512]{1,0:T(4,128)S(1)}, bf16[4,512,2048]{1,2,0:T(8,128)(2,1)}) fusion(pred[512,2048]{0,1:T(8,128)(4,1)S(1)} %copy-done.2, bf16[512,1,4,128]{3,2,1,0:T(4,128)(2,1)} %get-tuple-element.35, bf16[1536,128]{1,0:T(8,128)(2,1)} %bitcast.192, bf16[512,128]{1,0:T(8,128)(2,1)S(1)} %get-tuple-element.33), kind=kOutput, calls=%fused_computation.148 | convolution fusion | flops 1099958272 | bytes 10493952 | tf_op jit(solution)/shard_map/sub | solution.py:83
  301.6 5.9 %fusion.30 = bf16[512,4,128]{2,0,1:T(8,128)(2,1)S(1)} fusion(bf16[4,512,2048]{1,2,0:T(8,128)(2,1)} %get-tuple-element.72, bf16[1536,128]{1,0:T(8,128)(2,1)S(1)} %bitcast.190, bf16[512,128]{1,0:T(8,128)(2,1)S(1)} %get-tuple-element.30, f32[512,4]{0,1:T(4,128)S(1)} %bitcast.195), kind=kOutput, calls=%fused_computation.30 | convolution fusion | flops 1075314688 | bytes 9445376 | tf_op jit(solution)/shard_map/gqk,kd->gqd/dot_general | solution.py:86
  308.7 11.3 %fusion.61 = (f32[4,512]{1,0:T(4,128)S(1)}, bf16[4,512,2048]{1,2,0:T(8,128)(2,1)}) fusion(pred[512,2048]{0,1:T(8,128)(4,1)S(1)} %copy-done.1, bf16[512,1,4,128]{3,2,1,0:T(4,128)(2,1)S(1)} %get-tuple-element.36, bf16[1536,128]{1,0:T(8,128)(2,1)} %bitcast.191, bf16[512,128]{1,0:T(8,128)(2,1)S(1)} %get-tuple-element.34), kind=kOutput, calls=%fused_computation.147 | convolution fusion | flops 1099958272 | bytes 10493952 | tf_op jit(solution)/shard_map/sub | solution.py:83
  320.0 5.9 %fusion.33 = bf16[512,4,128]{2,0,1:T(8,128)(2,1)S(1)} fusion(bf16[4,512,2048]{1,2,0:T(8,128)(2,1)} %get-tuple-element.70, bf16[1536,128]{1,0:T(8,128)(2,1)S(1)} %bitcast.189, bf16[512,128]{1,0:T(8,128)(2,1)S(1)} %get-tuple-element.31, f32[512,4]{0,1:T(4,128)S(1)} %bitcast.196), kind=kOutput, calls=%fused_computation.31 | convolution fusion | flops 1075314688 | bytes 9445376 | tf_op jit(solution)/shard_map/gqk,kd->gqd/dot_general | solution.py:86
  326.7 19.9 %all_to_all.64 = bf16[4,128,1024]{2,1,0:T(8,128)(2,1)S(1)} all-to-all(bf16[4,128,1024]{2,1,0:T(8,128)(2,1)S(1)} %pad_maximum_fusion), channel_id=1, replica_groups=mesh['seq'=64,'head'=4] {'head'}, dimensions={0} | all-to-all | bytes 2097152 | tf_op jit(solution)/shard_map/all_to_all | solution.py:90
  (101 shorter events, 45.8 us)
Async XLA Ops:
  0.0 22.6 %copy-start = (bf16[128,4096]{1,0:T(8,128)(2,1)S(1)}, bf16[128,4096]{1,0:T(8,128)(2,1)}, u32[]{:S(2)}) copy-start(bf16[128,4096]{1,0:T(8,128)(2,1)} %param.4) | copy-start | bytes 3145732
  0.8 26.0 %collective-permute-start.22 = (s32[2,3]{1,0:T(2,128)S(1)}, s32[2,3]{1,0:T(2,128)S(1)}, u32[]{:S(2)}, u32[]{:S(2)}) collective-permute-start(s32[2,3]{1,0:T(2,128)S(1)} %add_bitcast_fusion), channel_id=1, source_target_pairs={{48,0},{52,4},{56,8},{60,12},{64,16},{68,20},{72,24},{76,28},{80,3... | collective-permute-start | bytes 80 | tf_op jit(solution)/shard_map/ppermute | solution.py:18
  3.9 26.8 %collective-permute-start.20 = (s32[2,3]{1,0:T(2,128)S(1)}, s32[2,3]{1,0:T(2,128)S(1)}, u32[]{:S(2)}, u32[]{:S(2)}) collective-permute-start(s32[2,3]{1,0:T(2,128)S(1)} %add_bitcast_fusion), channel_id=1, source_target_pairs={{44,0},{48,4},{52,8},{56,12},{60,16},{64,20},{68,24},{72,28},{76,3... | collective-permute-start | bytes 80 | tf_op jit(solution)/shard_map/ppermute | solution.py:18
  5.9 28.7 %collective-permute-start.18 = (s32[2,3]{1,0:T(2,128)S(1)}, s32[2,3]{1,0:T(2,128)S(1)}, u32[]{:S(2)}, u32[]{:S(2)}) collective-permute-start(s32[2,3]{1,0:T(2,128)S(1)} %add_bitcast_fusion), channel_id=1, source_target_pairs={{40,0},{44,4},{48,8},{52,12},{56,16},{60,20},{64,24},{68,28},{72,3... | collective-permute-start | bytes 80 | tf_op jit(solution)/shard_map/ppermute | solution.py:18
  8.7 31.0 %collective-permute-start.16 = (s32[2,3]{1,0:T(2,128)S(1)}, s32[2,3]{1,0:T(2,128)S(1)}, u32[]{:S(2)}, u32[]{:S(2)}) collective-permute-start(s32[2,3]{1,0:T(2,128)S(1)} %add_bitcast_fusion), channel_id=1, source_target_pairs={{36,0},{40,4},{44,8},{48,12},{52,16},{56,20},{60,24},{64,28},{68,3... | collective-permute-start | bytes 80 | tf_op jit(solution)/shard_map/ppermute | solution.py:18
  11.0 33.8 %collective-permute-start.14 = (s32[2,3]{1,0:T(2,128)S(1)}, s32[2,3]{1,0:T(2,128)S(1)}, u32[]{:S(2)}, u32[]{:S(2)}) collective-permute-start(s32[2,3]{1,0:T(2,128)S(1)} %add_bitcast_fusion), channel_id=1, source_target_pairs={{32,0},{36,4},{40,8},{44,12},{48,16},{52,20},{56,24},{60,28},{64,3... | collective-permute-start | bytes 80 | tf_op jit(solution)/shard_map/ppermute | solution.py:18
  14.6 50.7 %all-to-all-start = ((bf16[128,4,256]{2,0,1:T(8,128)(2,1)}), bf16[128,4,256]{2,0,1:T(8,128)(2,1)S(1)}, u32[]{:S(2)}, u32[]{:S(2)}) async-start(bf16[128,4,256]{2,0,1:T(8,128)(2,1)} %bitcast.182), calls=%async_computation | async-start | bytes 524288 | tf_op jit(solution)/shard_map/all_to_all | solution.py:24
  26.8 23.8 %collective-permute-start.12 = (s32[2,3]{1,0:T(2,128)S(1)}, s32[2,3]{1,0:T(2,128)S(1)}, u32[]{:S(2)}, u32[]{:S(2)}) collective-permute-start(s32[2,3]{1,0:T(2,128)S(1)} %add_bitcast_fusion), channel_id=1, source_target_pairs={{28,0},{32,4},{36,8},{40,12},{44,16},{48,20},{52,24},{56,28},{60,3... | collective-permute-start | bytes 80 | tf_op jit(solution)/shard_map/ppermute | solution.py:18
  30.7 24.3 %collective-permute-start.10 = (s32[2,3]{1,0:T(2,128)S(1)}, s32[2,3]{1,0:T(2,128)S(1)}, u32[]{:S(2)}, u32[]{:S(2)}) collective-permute-start(s32[2,3]{1,0:T(2,128)S(1)} %add_bitcast_fusion), channel_id=1, source_target_pairs={{24,0},{28,4},{32,8},{36,12},{40,16},{44,20},{48,24},{52,28},{56,3... | collective-permute-start | bytes 80 | tf_op jit(solution)/shard_map/ppermute | solution.py:18
  34.6 24.7 %collective-permute-start.8 = (s32[2,3]{1,0:T(2,128)S(1)}, s32[2,3]{1,0:T(2,128)S(1)}, u32[]{:S(2)}, u32[]{:S(2)}) collective-permute-start(s32[2,3]{1,0:T(2,128)S(1)} %add_bitcast_fusion), channel_id=1, source_target_pairs={{20,0},{24,4},{28,8},{32,12},{36,16},{40,20},{44,24},{48,28},{52,3... | collective-permute-start | bytes 80 | tf_op jit(solution)/shard_map/ppermute | solution.py:18
  39.8 21.5 %collective-permute-start.6 = (s32[2,3]{1,0:T(2,128)S(1)}, s32[2,3]{1,0:T(2,128)S(1)}, u32[]{:S(2)}, u32[]{:S(2)}) collective-permute-start(s32[2,3]{1,0:T(2,128)S(1)} %add_bitcast_fusion), channel_id=1, source_target_pairs={{16,0},{20,4},{24,8},{28,12},{32,16},{36,20},{40,24},{44,28},{48,3... | collective-permute-start | bytes 80 | tf_op jit(solution)/shard_map/ppermute | solution.py:18
  44.8 18.5 %collective-permute-start.4 = (s32[2,3]{1,0:T(2,128)S(1)}, s32[2,3]{1,0:T(2,128)S(1)}, u32[]{:S(2)}, u32[]{:S(2)}) collective-permute-start(s32[2,3]{1,0:T(2,128)S(1)} %add_bitcast_fusion), channel_id=1, source_target_pairs={{12,0},{16,4},{20,8},{24,12},{28,16},{32,20},{36,24},{40,28},{44,3... | collective-permute-start | bytes 80 | tf_op jit(solution)/shard_map/ppermute | solution.py:18
  50.6 19.5 %collective-permute-start.2 = (s32[2,3]{1,0:T(2,128)S(1)}, s32[2,3]{1,0:T(2,128)S(1)}, u32[]{:S(2)}, u32[]{:S(2)}) collective-permute-start(s32[2,3]{1,0:T(2,128)S(1)} %add_bitcast_fusion), channel_id=1, source_target_pairs={{8,0},{12,4},{16,8},{20,12},{24,16},{28,20},{32,24},{36,28},{40,32... | collective-permute-start | bytes 80 | tf_op jit(solution)/shard_map/ppermute | solution.py:18
  55.0 17.1 %collective-permute-start = (s32[2,3]{1,0:T(2,128)S(1)}, s32[2,3]{1,0:T(2,128)S(1)}, u32[]{:S(2)}, u32[]{:S(2)}) collective-permute-start(s32[2,3]{1,0:T(2,128)S(1)} %add_bitcast_fusion), channel_id=1, source_target_pairs={{4,0},{8,4},{12,8},{16,12},{20,16},{24,20},{28,24},{32,28},{36,32}... | collective-permute-start | bytes 80 | tf_op jit(solution)/shard_map/ppermute | solution.py:18
  65.3 11.8 %all-to-all-start.2 = ((bf16[128,4,256]{2,0,1:T(8,128)(2,1)}), bf16[128,4,256]{2,0,1:T(8,128)(2,1)S(1)}, u32[]{:S(2)}, u32[]{:S(2)}) async-start(bf16[128,4,256]{2,0,1:T(8,128)(2,1)} %bitcast.181), calls=%async_computation.2 | async-start | bytes 524288 | tf_op jit(solution)/shard_map/all_to_all | solution.py:25
  77.1 211.1 %all-to-all-start.1 = ((bf16[128,4,1024]{2,0,1:T(8,128)(2,1)}), bf16[128,4,1024]{2,0,1:T(8,128)(2,1)S(1)}, u32[]{:S(2)}, u32[]{:S(2)}) async-start(bf16[128,4,1024]{2,0,1:T(8,128)(2,1)} %bitcast.180), calls=%async_computation.1 | async-start | bytes 2097152 | tf_op jit(solution)/shard_map/all_to_all | solution.py:23
  81.1 134.3 %collective-permute-start.35 = (bf16[512,128]{1,0:T(8,128)(2,1)S(1)}, bf16[512,128]{1,0:T(8,128)(2,1)S(1)}, u32[]{:S(2)}, u32[]{:S(2)}) collective-permute-start(bf16[512,128]{1,0:T(8,128)(2,1)S(1)} %get-tuple-element.29), channel_id=1, source_target_pairs={{0,48},{4,52},{8,56},{12,60},{16,64},{20,68},{24,72},{28,76},{32,8... | collective-permute-start | bytes 393224 | tf_op jit(solution)/shard_map/ppermute | solution.py:18
  87.4 194.6 %collective-permute-start.23 = (bf16[512,128]{1,0:T(8,128)(2,1)}, bf16[512,128]{1,0:T(8,128)(2,1)S(1)}, u32[]{:S(2)}, u32[]{:S(2)}) collective-permute-start(bf16[512,128]{1,0:T(8,128)(2,1)} %get-tuple-element.32), channel_id=1, source_target_pairs={{0,48},{4,52},{8,56},{12,60},{16,64},{20,68},{24,72},{28,76},{32,8... | collective-permute-start | bytes 393224 | tf_op jit(solution)/shard_map/ppermute | solution.py:18
  94.5 126.1 %collective-permute-start.5 = (bf16[512,128]{1,0:T(8,128)(2,1)S(1)}, bf16[512,128]{1,0:T(8,128)(2,1)S(1)}, u32[]{:S(2)}, u32[]{:S(2)}) collective-permute-start(bf16[512,128]{1,0:T(8,128)(2,1)S(1)} %get-tuple-element.60), channel_id=1, source_target_pairs={{0,12},{4,16},{8,20},{12,24},{16,28},{20,32},{24,36},{28,40},{32,4... | collective-permute-start | bytes 393224 | tf_op jit(solution)/shard_map/ppermute | solution.py:18
  96.4 121.6 %collective-permute-start.3 = (bf16[512,128]{1,0:T(8,128)(2,1)S(1)}, bf16[512,128]{1,0:T(8,128)(2,1)S(1)}, u32[]{:S(2)}, u32[]{:S(2)}) collective-permute-start(bf16[512,128]{1,0:T(8,128)(2,1)S(1)} %get-tuple-element.61), channel_id=1, source_target_pairs={{0,8},{4,12},{8,16},{12,20},{16,24},{20,28},{24,32},{28,36},{32,40... | collective-permute-start | bytes 393224 | tf_op jit(solution)/shard_map/ppermute | solution.py:18
  100.1 6.7 %collective-permute-start.24 = (bf16[512,128]{1,0:T(8,128)(2,1)S(1)}, bf16[512,128]{1,0:T(8,128)(2,1)S(1)}, u32[]{:S(2)}, u32[]{:S(2)}) collective-permute-start(bf16[512,128]{1,0:T(8,128)(2,1)S(1)} %get-tuple-element.49), channel_id=1, source_target_pairs={{0,4},{4,8},{8,12},{12,16},{16,20},{20,24},{24,28},{28,32},{32,36}... | collective-permute-start | bytes 393224 | tf_op jit(solution)/shard_map/ppermute | solution.py:18
  106.7 6.3 %collective-permute-start.1 = (bf16[512,128]{1,0:T(8,128)(2,1)S(1)}, bf16[512,128]{1,0:T(8,128)(2,1)S(1)}, u32[]{:S(2)}, u32[]{:S(2)}) collective-permute-start(bf16[512,128]{1,0:T(8,128)(2,1)S(1)} %get-tuple-element.62), channel_id=1, source_target_pairs={{0,4},{4,8},{8,12},{12,16},{16,20},{20,24},{24,28},{28,32},{32,36}... | collective-permute-start | bytes 393224 | tf_op jit(solution)/shard_map/ppermute | solution.py:18
  113.0 12.9 %collective-permute-start.25 = (bf16[512,128]{1,0:T(8,128)(2,1)S(1)}, bf16[512,128]{1,0:T(8,128)(2,1)S(1)}, u32[]{:S(2)}, u32[]{:S(2)}) collective-permute-start(bf16[512,128]{1,0:T(8,128)(2,1)S(1)} %get-tuple-element.48), channel_id=1, source_target_pairs={{0,8},{4,12},{8,16},{12,20},{16,24},{20,28},{24,32},{28,36},{32,40... | collective-permute-start | bytes 393224 | tf_op jit(solution)/shard_map/ppermute | solution.py:18
  125.9 10.0 %collective-permute-start.26 = (bf16[512,128]{1,0:T(8,128)(2,1)S(1)}, bf16[512,128]{1,0:T(8,128)(2,1)S(1)}, u32[]{:S(2)}, u32[]{:S(2)}) collective-permute-start(bf16[512,128]{1,0:T(8,128)(2,1)S(1)} %get-tuple-element.47), channel_id=1, source_target_pairs={{0,12},{4,16},{8,20},{12,24},{16,28},{20,32},{24,36},{28,40},{32,4... | collective-permute-start | bytes 393224 | tf_op jit(solution)/shard_map/ppermute | solution.py:18
  135.9 11.0 %collective-permute-start.27 = (bf16[512,128]{1,0:T(8,128)(2,1)S(1)}, bf16[512,128]{1,0:T(8,128)(2,1)S(1)}, u32[]{:S(2)}, u32[]{:S(2)}) collective-permute-start(bf16[512,128]{1,0:T(8,128)(2,1)S(1)} %get-tuple-element.46), channel_id=1, source_target_pairs={{0,16},{4,20},{8,24},{12,28},{16,32},{20,36},{24,40},{28,44},{32,4... | collective-permute-start | bytes 393224 | tf_op jit(solution)/shard_map/ppermute | solution.py:18
  146.9 8.7 %collective-permute-start.28 = (bf16[512,128]{1,0:T(8,128)(2,1)S(1)}, bf16[512,128]{1,0:T(8,128)(2,1)S(1)}, u32[]{:S(2)}, u32[]{:S(2)}) collective-permute-start(bf16[512,128]{1,0:T(8,128)(2,1)S(1)} %get-tuple-element.45), channel_id=1, source_target_pairs={{0,20},{4,24},{8,28},{12,32},{16,36},{20,40},{24,44},{28,48},{32,5... | collective-permute-start | bytes 393224 | tf_op jit(solution)/shard_map/ppermute | solution.py:18
  155.6 10.4 %collective-permute-start.29 = (bf16[512,128]{1,0:T(8,128)(2,1)S(1)}, bf16[512,128]{1,0:T(8,128)(2,1)S(1)}, u32[]{:S(2)}, u32[]{:S(2)}) collective-permute-start(bf16[512,128]{1,0:T(8,128)(2,1)S(1)} %get-tuple-element.44), channel_id=1, source_target_pairs={{0,24},{4,28},{8,32},{12,36},{16,40},{20,44},{24,48},{28,52},{32,5... | collective-permute-start | bytes 393224 | tf_op jit(solution)/shard_map/ppermute | solution.py:18
  166.0 7.5 %collective-permute-start.30 = (bf16[512,128]{1,0:T(8,128)(2,1)S(1)}, bf16[512,128]{1,0:T(8,128)(2,1)S(1)}, u32[]{:S(2)}, u32[]{:S(2)}) collective-permute-start(bf16[512,128]{1,0:T(8,128)(2,1)S(1)} %get-tuple-element.43), channel_id=1, source_target_pairs={{0,28},{4,32},{8,36},{12,40},{16,44},{20,48},{24,52},{28,56},{32,6... | collective-permute-start | bytes 393224 | tf_op jit(solution)/shard_map/ppermute | solution.py:18
  173.4 9.4 %collective-permute-start.31 = (bf16[512,128]{1,0:T(8,128)(2,1)S(1)}, bf16[512,128]{1,0:T(8,128)(2,1)S(1)}, u32[]{:S(2)}, u32[]{:S(2)}) collective-permute-start(bf16[512,128]{1,0:T(8,128)(2,1)S(1)} %get-tuple-element.42), channel_id=1, source_target_pairs={{0,32},{4,36},{8,40},{12,44},{16,48},{20,52},{24,56},{28,60},{32,6... | collective-permute-start | bytes 393224 | tf_op jit(solution)/shard_map/ppermute | solution.py:18
  182.9 8.4 %collective-permute-start.32 = (bf16[512,128]{1,0:T(8,128)(2,1)S(1)}, bf16[512,128]{1,0:T(8,128)(2,1)S(1)}, u32[]{:S(2)}, u32[]{:S(2)}) collective-permute-start(bf16[512,128]{1,0:T(8,128)(2,1)S(1)} %get-tuple-element.41), channel_id=1, source_target_pairs={{0,36},{4,40},{8,44},{12,48},{16,52},{20,56},{24,60},{28,64},{32,6... | collective-permute-start | bytes 393224 | tf_op jit(solution)/shard_map/ppermute | solution.py:18
  191.2 9.0 %collective-permute-start.33 = (bf16[512,128]{1,0:T(8,128)(2,1)S(1)}, bf16[512,128]{1,0:T(8,128)(2,1)S(1)}, u32[]{:S(2)}, u32[]{:S(2)}) collective-permute-start(bf16[512,128]{1,0:T(8,128)(2,1)S(1)} %get-tuple-element.40), channel_id=1, source_target_pairs={{0,40},{4,44},{8,48},{12,52},{16,56},{20,60},{24,64},{28,68},{32,7... | collective-permute-start | bytes 393224 | tf_op jit(solution)/shard_map/ppermute | solution.py:18
  200.2 12.7 %collective-permute-start.34 = (bf16[512,128]{1,0:T(8,128)(2,1)S(1)}, bf16[512,128]{1,0:T(8,128)(2,1)S(1)}, u32[]{:S(2)}, u32[]{:S(2)}) collective-permute-start(bf16[512,128]{1,0:T(8,128)(2,1)S(1)} %get-tuple-element.39), channel_id=1, source_target_pairs={{0,44},{4,48},{8,52},{12,56},{16,60},{20,64},{24,68},{28,72},{32,7... | collective-permute-start | bytes 393224 | tf_op jit(solution)/shard_map/ppermute | solution.py:18
  212.9 68.5 %collective-permute-start.21 = (bf16[512,128]{1,0:T(8,128)(2,1)S(1)}, bf16[512,128]{1,0:T(8,128)(2,1)S(1)}, u32[]{:S(2)}, u32[]{:S(2)}) collective-permute-start(bf16[512,128]{1,0:T(8,128)(2,1)S(1)} %get-tuple-element.52), channel_id=1, source_target_pairs={{0,44},{4,48},{8,52},{12,56},{16,60},{20,64},{24,68},{28,72},{32,7... | collective-permute-start | bytes 393224 | tf_op jit(solution)/shard_map/ppermute | solution.py:18
  215.5 64.3 %collective-permute-start.19 = (bf16[512,128]{1,0:T(8,128)(2,1)S(1)}, bf16[512,128]{1,0:T(8,128)(2,1)}, u32[]{:S(2)}, u32[]{:S(2)}) collective-permute-start(bf16[512,128]{1,0:T(8,128)(2,1)S(1)} %get-tuple-element.53), channel_id=1, source_target_pairs={{0,40},{4,44},{8,48},{12,52},{16,56},{20,60},{24,64},{28,68},{32,7... | collective-permute-start | bytes 393224 | tf_op jit(solution)/shard_map/ppermute | solution.py:18
  218.0 56.3 %collective-permute-start.17 = (bf16[512,128]{1,0:T(8,128)(2,1)S(1)}, bf16[512,128]{1,0:T(8,128)(2,1)S(1)}, u32[]{:S(2)}, u32[]{:S(2)}) collective-permute-start(bf16[512,128]{1,0:T(8,128)(2,1)S(1)} %get-tuple-element.54), channel_id=1, source_target_pairs={{0,36},{4,40},{8,44},{12,48},{16,52},{20,56},{24,60},{28,64},{32,6... | collective-permute-start | bytes 393224 | tf_op jit(solution)/shard_map/ppermute | solution.py:18
  220.6 18.1 %collective-permute-start.7 = (bf16[512,128]{1,0:T(8,128)(2,1)S(1)}, bf16[512,128]{1,0:T(8,128)(2,1)S(1)}, u32[]{:S(2)}, u32[]{:S(2)}) collective-permute-start(bf16[512,128]{1,0:T(8,128)(2,1)S(1)} %get-tuple-element.59), channel_id=1, source_target_pairs={{0,16},{4,20},{8,24},{12,28},{16,32},{20,36},{24,40},{28,44},{32,4... | collective-permute-start | bytes 393224 | tf_op jit(solution)/shard_map/ppermute | solution.py:18
  238.7 8.4 %collective-permute-start.9 = (bf16[512,128]{1,0:T(8,128)(2,1)S(1)}, bf16[512,128]{1,0:T(8,128)(2,1)S(1)}, u32[]{:S(2)}, u32[]{:S(2)}) collective-permute-start(bf16[512,128]{1,0:T(8,128)(2,1)S(1)} %get-tuple-element.58), channel_id=1, source_target_pairs={{0,20},{4,24},{8,28},{12,32},{16,36},{20,40},{24,44},{28,48},{32,5... | collective-permute-start | bytes 393224 | tf_op jit(solution)/shard_map/ppermute | solution.py:18
  247.1 9.8 %collective-permute-start.11 = (bf16[512,128]{1,0:T(8,128)(2,1)S(1)}, bf16[512,128]{1,0:T(8,128)(2,1)S(1)}, u32[]{:S(2)}, u32[]{:S(2)}) collective-permute-start(bf16[512,128]{1,0:T(8,128)(2,1)S(1)} %get-tuple-element.57), channel_id=1, source_target_pairs={{0,24},{4,28},{8,32},{12,36},{16,40},{20,44},{24,48},{28,52},{32,5... | collective-permute-start | bytes 393224 | tf_op jit(solution)/shard_map/ppermute | solution.py:18
  257.0 7.5 %collective-permute-start.13 = (bf16[512,128]{1,0:T(8,128)(2,1)S(1)}, bf16[512,128]{1,0:T(8,128)(2,1)S(1)}, u32[]{:S(2)}, u32[]{:S(2)}) collective-permute-start(bf16[512,128]{1,0:T(8,128)(2,1)S(1)} %get-tuple-element.56), channel_id=1, source_target_pairs={{0,28},{4,32},{8,36},{12,40},{16,44},{20,48},{24,52},{28,56},{32,6... | collective-permute-start | bytes 393224 | tf_op jit(solution)/shard_map/ppermute | solution.py:18
  264.4 9.2 %collective-permute-start.15 = (bf16[512,128]{1,0:T(8,128)(2,1)S(1)}, bf16[512,128]{1,0:T(8,128)(2,1)S(1)}, u32[]{:S(2)}, u32[]{:S(2)}) collective-permute-start(bf16[512,128]{1,0:T(8,128)(2,1)S(1)} %get-tuple-element.55), channel_id=1, source_target_pairs={{0,32},{4,36},{8,40},{12,44},{16,48},{20,52},{24,56},{28,60},{32,6... | collective-permute-start | bytes 393224 | tf_op jit(solution)/shard_map/ppermute | solution.py:18
  289.0 1.2 copy-start.2
  290.2 11.4 %copy-start.3 = (bf16[3,512,128]{2,1,0:T(8,128)(2,1)S(1)}, bf16[3,512,128]{2,1,0:T(8,128)(2,1)}, u32[]{:S(2)}) copy-start(bf16[3,512,128]{2,1,0:T(8,128)(2,1)} %gather_fusion.1) | copy-start | bytes 1179652
  307.5 1.2 copy-start.1
where the time goes:
time: 351 us; the launch traced here: 349 us
  waiting for transfers between devices  122 us (35%)
  starting transfers between devices  103 us (29%)
  local copies, waits for them, and re-layouts  38.3 us (11%)
  matrix products  34.5 us (10%)
  blocking collectives  19.9 us (6%)
  between operations  15.8 us (5%)
  other arithmetic  15.2 us (4%)
    ppermute x36, waiting for transfers between devices, shifted(): return lax.ppermute(value, axis, pairs)  119 us
    ppermute x36, starting transfers between devices, shifted(): return lax.ppermute(value, axis, pairs)  89.8 us
    sub x2, matrix products, on_device(): expo = jnp.where(mask, jnp.exp(score - top), 0.0)  22.6 us
    all_to_all x1, blocking collectives, on_device(): lax.all_to_all(local_out, 'head', split_axis=0, concat_axis=1, tiled=True)  19.9 us
    unnamed x30, local copies, waits for them, and re-layouts  16.1 us
    dot_general x2, matrix products, on_device(): jnp.einsum('gqk,kd->gqd', weight, val_cat, preferred_element_type=jnp.flo...  11.9 us
    reduce_or x12, other arithmetic, on_device(): named = jnp.any(their[local_head] == mine + 1)  8.58 us
  transfers between devices with their start and end apart: 39, of which 18 were waited for; matrix products, arithmetic and copies ran while one was open for 13% of the time, Pallas kernels for 0%

commit v1 on v0

v1 whole, which is shorter than its diff:
```python
import math

import jax
import jax.numpy as jnp
from jax import lax
from jax.experimental import pallas as pl
from jax.experimental.pallas import tpu as pltpu
from jax.sharding import PartitionSpec as P

HQ = 32
HK = 8
DH = 128
BLK = 512
TOPK = 3
GRP = HQ // HK
NHEAD = 4
HLOC = HK // NHEAD
TOK = BLK // NHEAD
NX = 4
SLOTS = 13
GROUPS = 2 * HLOC
PARTS = 2
PIECES = GROUPS * PARTS
ROWS = BLK // PARTS
WIDE = GRP * DH
NEG = -1e30
RATE = math.log2(math.e) / math.sqrt(DH)
MESH = pl.DeviceIdType.MESH


def kernel(nseq, chosen, query, keys, values, out, kv0, kv1, kv2, kv3, qbuf, obuf, scores, weights, totals,
           own_send, own_recv, q_send, q_recv, win_send, win_recv, sib_send, sib_recv,
           out_send, out_recv, local_sem):
    kv = (kv0, kv1, kv2, kv3)
    nz = nseq // (2 * NX)
    seq = lax.axis_index("seq")
    y = lax.axis_index("head")
    core = lax.rem(seq, 2)
    x = lax.rem(seq // 2, NX)
    z = seq // (2 * NX)

    def at(zz, xx):
        return ((zz * NX + xx) * 2 + core, y)

    up = at(lax.rem(z + 1, nz), x)
    down = at(lax.rem(z + nz - 1, nz), x)
    right = at(z, lax.rem(x + 1, NX))
    left = at(z, lax.rem(x + NX - 1, NX))
    sibling = (seq + 1 - 2 * core, y)

    def partner(o):
        return (seq, lax.rem(y + o, NHEAD))

    barrier = pltpu.get_barrier_semaphore()
    for who in [up, down, right, left, sibling, partner(1), partner(2), partner(3)]:
        pl.semaphore_signal(barrier, inc=1, device_id=who, device_id_type=MESH)
    pl.semaphore_wait(barrier, 8)

    def columns(start, width):
        return pl.ds(pl.multiple_of(start, DH), width)

    def remote(src, dst, send, recv, to):
        return pltpu.make_async_remote_copy(
            src_ref=src, dst_ref=dst, send_sem=send, recv_sem=recv, device_id=to, device_id_type=MESH)

    own_rows = pl.ds(pl.multiple_of(y * TOK, TOK), TOK)

    def kv_source(g, to_y):
        return (keys, values)[g % 2].at[:, columns((to_y * HLOC + g // 2) * DH, DH)]

    def kv_copy(o, g):
        to = partner(o)
        return remote(kv_source(g, to[1]), kv[g].at[0, own_rows], own_send.at[g], own_recv.at[g], to)

    def kv_local(g):
        return pltpu.make_async_copy(kv_source(g, y), kv[g].at[0, own_rows], local_sem.at[g])

    def q_source(h, to_y):
        return query.at[:, columns((to_y * HLOC + h) * WIDE, WIDE)]

    def q_copy(o, h):
        to = partner(o)
        return remote(q_source(h, to[1]), qbuf.at[h, y], q_send.at[h], q_recv.at[h], to)

    def q_local(h):
        return pltpu.make_async_copy(q_source(h, y), qbuf.at[h, y], local_sem.at[GROUPS + h])

    def out_place(to_y, h):
        return out.at[:, columns((to_y * HLOC + h) * WIDE, WIDE)]

    def out_copy(o, h):
        to = partner(o)
        return remote(obuf.at[h, to[1]], out_place(y, h), out_send.at[h], out_recv.at[h], to)

    def out_local(h):
        return pltpu.make_async_copy(obuf.at[h, y], out_place(y, h), local_sem.at[GROUPS + HLOC + h])

    def three(ref, send, recv):
        return remote(ref, ref, send, recv, sibling)

    def kv_three(g):
        return three(kv[g].at[0, pl.ds(0, 3 * TOK)], own_send.at[g], own_recv.at[g])

    def q_three(h):
        return three(qbuf.at[h, pl.ds(0, 3)], q_send.at[h], q_recv.at[h])

    def out_three(h):
        return three(obuf.at[h, pl.ds(0, 3)], out_send.at[h], out_recv.at[h])

    def send_q(h):
        for o in (2, 1, 3):
            q_copy(o, h).start()
        q_local(h).start()

    def piece(m, slot):
        return kv[m // PARTS].at[slot, pl.ds((m % PARTS) * ROWS, ROWS)]

    def forward(m, to, r, into):
        remote(piece(m, 2 * r), piece(m, 2 * into),
               win_send.at[m // PARTS], win_recv.at[m, into - 1], to).start()

    def arrived(m, r):
        remote(piece(m, 2 * r), piece(m, 2 * r), win_send.at[m // PARTS], win_recv.at[m, r - 1], up).wait_recv()

    def share(m, r):
        g = m // PARTS

        def go():
            remote(piece(m, 2 * r), piece(m, 2 * r + 1 - 2 * core), sib_send.at[g], sib_recv.at[g], sibling).start()

        if r == 0:
            pl.when(core == 0)(go)
        elif r == 6:
            pl.when(core == 1)(go)
        else:
            go()

    def when(cond, *args):
        pl.when(cond)(lambda: forward(*args))

    def lag0(m):
        if m % PARTS == 0:
            kv_three(m // PARTS).wait_recv()
            kv_local(m // PARTS).wait()
        forward(m, up, 0, 4)
        when(x < 3, m, right, 0, 1)
        when(x == 0, m, left, 0, 3)
        share(m, 0)

    def lag1(m):
        arrived(m, 4)
        when(x > 0, m, left, 4, 3)
        when(x == 3, m, right, 4, 1)
        when(x < 2, m, right, 4, 5)
        share(m, 4)

        @pl.when(x == 3)
        def _():
            arrived(m, 3)
            forward(m, left, 3, 2)
            share(m, 3)

        @pl.when(x > 0)
        def _():
            arrived(m, 1)
            when(x == 2, m, right, 1, 2)
            when(x == 3, m, up, 1, 5)
            share(m, 1)

    def lag2(m):
        @pl.when(x == 0)
        def _():
            arrived(m, 1)
            share(m, 1)

        @pl.when(x < 3)
        def _():
            arrived(m, 3)
            when(x == 0, m, left, 3, 6)
            when(x == 2, m, left, 3, 2)
            share(m, 3)

        @pl.when(x == 3)
        def _():
            arrived(m, 5)
            forward(m, right, 5, 2)
            share(m, 5)
            arrived(m, 2)
            share(m, 2)

        @pl.when(x == 2)
        def _():
            arrived(m, 2)
            forward(m, up, 2, 6)
            share(m, 2)

        @pl.when((x == 1) | (x == 2))
        def _():
            arrived(m, 5)
            share(m, 5)

    def lag3(m):
        @pl.when(x < 2)
        def _():
            arrived(m, 2)
            forward(m, up, 2, 6)
            share(m, 2)

        @pl.when(x >= 2)
        def _():
            arrived(m, 6)
            share(m, 6)

    def lag4(m):
        @pl.when(x < 2)
        def _():
            arrived(m, 6)
            when(x == 1, m, left, 6, 5)
            share(m, 6)

    def lag5(m):
        @pl.when(x == 0)
        def _():
            arrived(m, 5)
            share(m, 5)

    lags = [lag0, lag1, lag2, lag3, lag4, lag5]

    def step(n):
        for lag, event in enumerate(lags):
            if 0 <= n - lag < PIECES:
                event(n - lag)

    for g in range(GROUPS):
        for o in (2, 1, 3):
            kv_copy(o, g).start()
        kv_local(g).start()

    done = PARTS - 1 + len(lags) - 1
    for n in range(done + 1):
        step(n)
        if n == 1:
            send_q(0)
        if n == 4:
            send_q(1)

    token = lax.rem(lax.broadcasted_iota(jnp.int32, (GRP * TOK, BLK), 0), TOK)
    key_at = lax.broadcasted_iota(jnp.int32, (GRP * TOK, BLK), 1)

    def whole(g):
        ref = kv[g].at[pl.ds(0, 6)]
        return remote(ref, ref, sib_send.at[g], sib_recv.at[g], sibling)

    def picks(h):
        valid, slot = [None], [0]
        for t in range(TOPK):
            pick = chosen[0, h, t]
            valid.append(pick >= 0)
            slot.append(jnp.where(pick >= 0, jnp.clip(seq - pick, 0, SLOTS - 1), 0))
        return valid, slot

    def weigh(h, c):
        wide = qbuf[h, c]
        q = jnp.concatenate([wide[:, g * DH:(g + 1) * DH] for g in range(GRP)], axis=0)
        valid, slot = picks(h)
        top = None
        for t in range(TOPK + 1):
            s = lax.dot_general(q, kv[2 * h][slot[t]], (((1,), (1,)), ((), ())),
                                preferred_element_type=jnp.float32)
            if t == 0:
                s = jnp.where(token + c * TOK >= key_at, s, NEG)
            scores[t] = s
            high = jnp.max(s, axis=1, keepdims=True)
            top = high if t == 0 else jnp.maximum(top, jnp.where(valid[t], high, NEG))
        total = None
        for t in range(TOPK + 1):
            shift = top if t == 0 else jnp.where(valid[t], top, -NEG)
            p = jnp.exp2((scores[t] - shift) * RATE)
            add = jnp.sum(p, axis=1, keepdims=True)
            weights[c, t] = p.astype(jnp.bfloat16)
            total = add if t == 0 else total + add
        totals[c] = jnp.broadcast_to(total, (GRP * TOK, DH))

    def attend(h, c, o):
        _, slot = picks(h)
        acc = None
        for t in range(TOPK + 1):
            part = lax.dot_general(weights[c, t], kv[2 * h + 1][slot[t]], (((1,), (0,)), ((), ())),
                                   preferred_element_type=jnp.float32)
            acc = part if t == 0 else acc + part
        res = (acc / totals[c]).astype(jnp.bfloat16)
        for g in range(GRP):
            obuf[h, c, :, g * DH:(g + 1) * DH] = res[g * TOK:(g + 1) * TOK]
        for k in (1, 2, 3):
            pl.when(o == k)(lambda: out_copy(k, h).start())
        pl.when(o == 0)(lambda: out_local(h).start())

    def phase(h, work, steps):
        def body(j, _):
            o = lax.rem(j + 1, NHEAD)
            work(h, lax.rem(y + o, NHEAD), o)
            for after, n in steps:
                pl.when(j == after)(lambda: step(n))
            return 0

        lax.fori_loop(0, NHEAD, body, 0)

    def weigh_phase(h, steps):
        whole(2 * h).wait_recv()
        q_three(h).wait_recv()
        q_local(h).wait()
        phase(h, lambda h, c, o: weigh(h, c), steps)

    def attend_phase(h, steps):
        whole(2 * h + 1).wait_recv()
        phase(h, attend, steps)

    weigh_phase(0, [(0, done + 1), (2, done + 2)])
    attend_phase(0, [(1, done + 3), (3, done + 4)])
    weigh_phase(1, [(0, done + 5), (2, done + 6)])
    attend_phase(1, [])

    for g in range(GROUPS):
        kv_three(g).wait_send()
        whole(g).wait_send()
        ref = kv[g].at[pl.ds(0, 6)]
        remote(ref, ref, win_send.at[g], sib_recv.at[g], up).wait_send()
    for h in range(HLOC):
        q_three(h).wait_send()
        out_three(h).wait()
        out_local(h).wait()


def on_device(query, keys, values, chosen):
    nseq = lax.axis_size("seq")
    dma = pltpu.SemaphoreType.DMA
    any_spec = pl.BlockSpec(memory_space=pl.ANY)

    def body(*refs):
        kernel(nseq, *refs)

    return pl.pallas_call(
        body,
        out_shape=jax.ShapeDtypeStruct(query.shape, jnp.bfloat16),
        in_specs=[pl.BlockSpec(memory_space=pltpu.SMEM), any_spec, any_spec, any_spec],
        out_specs=any_spec,
        scratch_shapes=[pltpu.VMEM((SLOTS, BLK, DH), jnp.bfloat16)] * GROUPS + [
            pltpu.VMEM((HLOC, NHEAD, TOK, WIDE), jnp.bfloat16),
            pltpu.VMEM((HLOC, NHEAD, TOK, WIDE), jnp.bfloat16),
            pltpu.VMEM((TOPK + 1, GRP * TOK, BLK), jnp.float32),
            pltpu.VMEM((NHEAD, TOPK + 1, GRP * TOK, BLK), jnp.bfloat16),
            pltpu.VMEM((NHEAD, GRP * TOK, DH), jnp.float32),
            dma((GROUPS,)), dma((GROUPS,)),
            dma((HLOC,)), dma((HLOC,)),
            dma((GROUPS,)), dma((PIECES, 6)),
            dma((GROUPS,)), dma((GROUPS,)),
            dma((HLOC,)), dma((HLOC,)),
            dma((GROUPS + 2 * HLOC,)),
        ],
        compiler_params=pltpu.CompilerParams(
            collective_id=0, has_side_effects=True, vmem_limit_bytes=56 * 1024 * 1024),
        cost_estimate=pl.CostEstimate(
            flops=4 * BLK * HLOC * GRP * BLK * 4 * DH, bytes_accessed=4 * 1024 * 1024,
            transcendentals=HLOC * GRP * BLK * BLK * 4),
        name="window_attention",
    )(chosen, query, keys, values)


def solution(mesh):
    in_specs = (
        P(("seq", "head"), None),
        P(("seq", "head"), None),
        P(("seq", "head"), None),
        P("seq", "head", None),
    )
    return jax.shard_map(
        on_device, mesh=mesh, in_specs=in_specs, out_specs=P(("seq", "head"), None), check_vma=False
    )
```

time: 351 us -> 70.7 us (0.20)
  the two profiles are of different devices: /device:TPU:130 before, /device:TPU:1 now
where the time goes in v1:
time: 70.7 us; the launch traced here: 70.6 us
  Pallas kernels  68.3 us (97%)
  local copies, waits for them, and re-layouts  2.29 us (3%)
    pallas_call x1, Pallas kernels, on_device(): pl.pallas_call(body, out_shape=jax.ShapeDtypeStruct(query.shape, jnp.bflo...  68.3 us
    unnamed x1, local copies, waits for them, and re-layouts  2.29 us

profile of v1, /device:TPU:1, one launch (start us, length us, event | category | flops | bytes accessed | tf_op | source)
XLA Modules:
  0.0 70.6 jit_solution(17913763887487125831)
XLA Ops:
  0.0 68.3 %window_attention.1 = bf16[128,4096]{1,0:T(8,128)(2,1)} custom-call(s32[1,2,3]{2,1,0:T(2,128)} %refs_0_.1, bf16[128,4096]{1,0:T(8,128)(2,1)} %refs_1_.1, bf16[128,1024]{1,0:T(8,128)(2,1)} %refs_2_.1, bf16[128,1024]{1,0:T(8,128)(2,1)} %refs_3_.1), custom_call_target="tpu_custom_call" | custom-call | flops 4294967296 | bytes 4194304 | tf_op jit(solution)/shard_map/window_attention/pallas_call | solution.py:342
  68.3 2.3 %copy.6 = bf16[128,4096]{1,0:T(8,128)(2,1)} copy(bf16[128,4096]{1,0:T(8,128)(2,1)} %window_attention.1) | data formatting | bytes 2097152

commit v2 on v1

--- a/solution.py
+++ b/solution.py
@@ -23,12 +23,15 @@
 PIECES = GROUPS * PARTS
 ROWS = BLK // PARTS
 WIDE = GRP * DH
+TILE = 256
+TILES = (TOPK + 1) * BLK // TILE
+BAND = GRP * TOK // TILES
 NEG = -1e30
 RATE = math.log2(math.e) / math.sqrt(DH)
 MESH = pl.DeviceIdType.MESH
 
 
-def kernel(nseq, chosen, query, keys, values, out, kv0, kv1, kv2, kv3, qbuf, obuf, scores, weights, totals,
+def kernel(nseq, chosen, query, keys, values, out, kv0, kv1, kv2, kv3, qbuf, obuf, scores_a, scores_b, weights, totals,
            own_send, own_recv, q_send, q_recv, win_send, win_recv, sib_send, sib_recv,
            out_send, out_recv, local_sem):
     kv = (kv0, kv1, kv2, kv3)
@@ -244,81 +247,107 @@
         if n == 4:
             send_q(1)
 
-    token = lax.rem(lax.broadcasted_iota(jnp.int32, (GRP * TOK, BLK), 0), TOK)
-    key_at = lax.broadcasted_iota(jnp.int32, (GRP * TOK, BLK), 1)
-
     def whole(g):
         ref = kv[g].at[pl.ds(0, 6)]
         return remote(ref, ref, sib_send.at[g], sib_recv.at[g], sibling)
 
-    def picks(h):
-        valid, slot = [None], [0]
-        for t in range(TOPK):
-            pick = chosen[0, h, t]
-            valid.append(pick >= 0)
-            slot.append(jnp.where(pick >= 0, jnp.clip(seq - pick, 0, SLOTS - 1), 0))
-        return valid, slot
-
-    def weigh(h, c):
-        wide = qbuf[h, c]
+    def offset(j):
+        return (j + 1) % NHEAD
+
+    def chunk(j):
+        return lax.rem(y + offset(j), NHEAD)
+
+    def pick(h, t):
+        named = chosen[0, h, t]
+        return named >= 0, jnp.where(named >= 0, jnp.clip(seq - named, 0, SLOTS - 1), 0)
+
+    ahead = (lax.broadcasted_iota(jnp.int32, (BAND, TILE), 0)
+             - lax.broadcasted_iota(jnp.int32, (BAND, TILE), 1))
+
+    def multiply(h, j, i, into):
+        wide = qbuf[h, chunk(j)]
         q = jnp.concatenate([wide[:, g * DH:(g + 1) * DH] for g in range(GRP)], axis=0)
-        valid, slot = picks(h)
+        t = i // 2
+        slot = jnp.where(t == 0, 0, pick(h, jnp.maximum(t - 1, 0))[1])
+        k = kv[2 * h][slot, pl.ds(pl.multiple_of(lax.rem(i, 2) * TILE, TILE), TILE)]
+        into[i] = lax.dot_general(q, k, (((1,), (1,)), ((), ())), preferred_element_type=jnp.float32)
+
+    def normalize(h, j, i, source):
+        c = chunk(j)
+        rows = pl.ds(pl.multiple_of(i * BAND, BAND), BAND)
+        first = c * TOK + lax.rem(i * BAND, TOK)
+
+        def tile(u):
+            s = source[u, rows]
+            if u * TILE < BLK:
+                s = jnp.where(ahead >= u * TILE - first, s, NEG)
+            return s
+
+        valid = [None] + [pick(h, t)[0] for t in range(TOPK)]
         top = None
         for t in range(TOPK + 1):
-            s = lax.dot_general(q, kv[2 * h][slot[t]], (((1,), (1,)), ((), ())),
-                                preferred_element_type=jnp.float32)
-            if t == 0:
-                s = jnp.where(token + c * TOK >= key_at, s, NEG)
-            scores[t] = s
-            high = jnp.max(s, axis=1, keepdims=True)
+            high = None
+            for u in (2 * t, 2 * t + 1):
+                s = tile(u)
+                s = jnp.maximum(s[:, :DH], s[:, DH:])
+                high = s if high is None else jnp.maximum(high, s)
             top = high if t == 0 else jnp.maximum(top, jnp.where(valid[t], high, NEG))
+        top = jnp.max(top, axis=1, keepdims=True)
         total = None
         for t in range(TOPK + 1):
             shift = top if t == 0 else jnp.where(valid[t], top, -NEG)
-            p = jnp.exp2((scores[t] - shift) * RATE)
-            add = jnp.sum(p, axis=1, keepdims=True)
-            weights[c, t] = p.astype(jnp.bfloat16)
-            total = add if t == 0 else total + add
-        totals[c] = jnp.broadcast_to(total, (GRP * TOK, DH))
-
-    def attend(h, c, o):
-        _, slot = picks(h)
+            for u in (2 * t, 2 * t + 1):
+                p = jnp.exp2((tile(u) - shift) * RATE)
+                weights[c, rows, u * TILE:(u + 1) * TILE] = p.astype(jnp.bfloat16)
+                p = p[:, :DH] + p[:, DH:]
+                total = p if total is None else total + p
+        totals[c, rows] = jnp.broadcast_to(jnp.sum(total, axis=1, keepdims=True), (BAND, DH))
+
+    def attend(h, j):
+        c = chunk(j)
         acc = None
         for t in range(TOPK + 1):
-            part = lax.dot_general(weights[c, t], kv[2 * h + 1][slot[t]], (((1,), (0,)), ((), ())),
-                                   preferred_element_type=jnp.float32)
+            slot = 0 if t == 0 else pick(h, t - 1)[1]
+            part = lax.dot_general(weights[c, :, t * BLK:(t + 1) * BLK], kv[2 * h + 1][slot],
+                                   (((1,), (0,)), ((), ())), preferred_element_type=jnp.float32)
             acc = part if t == 0 else acc + part
         res = (acc / totals[c]).astype(jnp.bfloat16)
         for g in range(GRP):
             obuf[h, c, :, g * DH:(g + 1) * DH] = res[g * TOK:(g + 1) * TOK]
-        for k in (1, 2, 3):
-            pl.when(o == k)(lambda: out_copy(k, h).start())
-        pl.when(o == 0)(lambda: out_local(h).start())
-
-    def phase(h, work, steps):
-        def body(j, _):
-            o = lax.rem(j + 1, NHEAD)
-            work(h, lax.rem(y + o, NHEAD), o)
-            for after, n in steps:
-                pl.when(j == after)(lambda: step(n))
-            return 0
-
-        lax.fori_loop(0, NHEAD, body, 0)
+        if offset(j) == 0:
+            out_local(h).start()
+        else:
+            out_copy(offset(j), h).start()
+
+    sides = (scores_a, scores_b)
 
     def weigh_phase(h, steps):
         whole(2 * h).wait_recv()
         q_three(h).wait_recv()
         q_local(h).wait()
-        phase(h, lambda h, c, o: weigh(h, c), steps)
+        for j in range(NHEAD + 1):
+            def body(i, _):
+                if j > 0:
+                    normalize(h, j - 1, i, sides[(j - 1) % 2])
+                if j < NHEAD:
+                    multiply(h, j, i, sides[j % 2])
+                return 0
+
+            lax.fori_loop(0, TILES, body, 0)
+            if j in steps:
+                step(steps[j])
 
     def attend_phase(h, steps):
         whole(2 * h + 1).wait_recv()
-        phase(h, attend, steps)
-
-    weigh_phase(0, [(0, done + 1), (2, done + 2)])
-    attend_phase(0, [(1, done + 3), (3, done + 4)])
-    weigh_phase(1, [(0, done + 5), (2, done + 6)])
-    attend_phase(1, [])
+        for j in range(NHEAD):
+            attend(h, j)
+            if j in steps:
+                step(steps[j])
+
+    weigh_phase(0, {0: done + 1, 2: done + 2})
+    attend_phase(0, {1: done + 3, 3: done + 4})
+    weigh_phase(1, {0: done + 5, 2: done + 6})
+    attend_phase(1, {})
 
     for g in range(GROUPS):
         kv_three(g).wait_send()
@@ -341,14 +370,15 @@
 
     return pl.pallas_call(
         body,
-        out_shape=jax.ShapeDtypeStruct(query.shape, jnp.bfloat16),
+        out_shape=pltpu.VMEM(query.shape, jnp.bfloat16),
         in_specs=[pl.BlockSpec(memory_space=pltpu.SMEM), any_spec, any_spec, any_spec],
-        out_specs=any_spec,
+        out_specs=pl.BlockSpec(memory_space=pltpu.VMEM),
         scratch_shapes=[pltpu.VMEM((SLOTS, BLK, DH), jnp.bfloat16)] * GROUPS + [
             pltpu.VMEM((HLOC, NHEAD, TOK, WIDE), jnp.bfloat16),
             pltpu.VMEM((HLOC, NHEAD, TOK, WIDE), jnp.bfloat16),
-            pltpu.VMEM((TOPK + 1, GRP * TOK, BLK), jnp.float32),
-            pltpu.VMEM((NHEAD, TOPK + 1, GRP * TOK, BLK), jnp.bfloat16),
+            pltpu.VMEM((TILES, GRP * TOK, TILE), jnp.float32),
+            pltpu.VMEM((TILES, GRP * TOK, TILE), jnp.float32),
+            pltpu.VMEM((NHEAD, GRP * TOK, (TOPK + 1) * BLK), jnp.bfloat16),
             pltpu.VMEM((NHEAD, GRP * TOK, DH), jnp.float32),
             dma((GROUPS,)), dma((GROUPS,)),
             dma((HLOC,)), dma((HLOC,)),

time: 70.7 us -> 78.3 us (1.11)
  Pallas kernels: 68.3 us -> 77.3 us
  local copies, waits for them, and re-layouts: 2.29 us -> 0.97 us
    pallas_call x1, Pallas kernels: 68.3 us -> 77.3 us  [on_device(): pl.pallas_call(body, out_shape=pltpu.VMEM(query.shape, jnp.bfloat16), in_...]
    unnamed x1, local copies, waits for them, and re-layouts: 2.29 us -> 0.97 us
where the time goes in v2:
time: 78.3 us; the launch traced here: 78.2 us
  Pallas kernels  77.3 us (99%)
  local copies, waits for them, and re-layouts  0.97 us (1%)
    pallas_call x1, Pallas kernels, on_device(): pl.pallas_call(body, out_shape=pltpu.VMEM(query.shape, jnp.bfloat16), in_...  77.3 us

profile of v2, /device:TPU:1, one launch (start us, length us, event | category | flops | bytes accessed | tf_op | source)
XLA Modules:
  0.0 78.2 jit_solution(5590241472714882153)
XLA Ops:
  0.0 77.3 %window_attention.1 = bf16[128,4096]{1,0:T(8,128)(2,1)S(1)} custom-call(s32[1,2,3]{2,1,0:T(2,128)} %refs_0_.1, bf16[128,4096]{1,0:T(8,128)(2,1)} %refs_1_.1, bf16[128,1024]{1,0:T(8,128)(2,1)} %refs_2_.1, bf16[128,1024]{1,0:T(8,128)(2,1)} %refs_3_.1), custom_call_target="tpu_custom_call" | custom-call | flops 4294967296 | bytes 4194304 | tf_op jit(solution)/shard_map/window_attention/pallas_call | solution.py:371
  77.3 1.0 %copy.6 = bf16[128,4096]{1,0:T(8,128)(2,1)} copy(bf16[128,4096]{1,0:T(8,128)(2,1)S(1)} %window_attention.1) | data formatting | bytes 2097152

commit v3 on v1

--- a/solution.py
+++ b/solution.py
@@ -28,7 +28,7 @@
 MESH = pl.DeviceIdType.MESH
 
 
-def kernel(nseq, chosen, query, keys, values, out, kv0, kv1, kv2, kv3, qbuf, obuf, scores, weights, totals,
+def kernel(nseq, chosen, query, keys, values, out, kv0, kv1, kv2, kv3, qbuf, obuf, scores, weights, totals, flipped,
            own_send, own_recv, q_send, q_recv, win_send, win_recv, sib_send, sib_recv,
            out_send, out_recv, local_sem):
     kv = (kv0, kv1, kv2, kv3)
@@ -126,8 +126,10 @@
         g = m // PARTS
 
         def go():
-            remote(piece(m, 2 * r), piece(m, 2 * r + 1 - 2 * core), sib_send.at[g], sib_recv.at[g], sibling).start()
-
+            remote(kv[g].at[2 * r], kv[g].at[2 * r + 1 - 2 * core], sib_send.at[g], sib_recv.at[g], sibling).start()
+
+        if m % PARTS < PARTS - 1:
+            return
         if r == 0:
             pl.when(core == 0)(go)
         elif r == 6:
@@ -244,8 +246,8 @@
         if n == 4:
             send_q(1)
 
-    token = lax.rem(lax.broadcasted_iota(jnp.int32, (GRP * TOK, BLK), 0), TOK)
-    key_at = lax.broadcasted_iota(jnp.int32, (GRP * TOK, BLK), 1)
+    key_at = lax.broadcasted_iota(jnp.int32, (BLK, GRP * TOK), 0)
+    token = lax.rem(lax.broadcasted_iota(jnp.int32, (BLK, GRP * TOK), 1), TOK)
 
     def whole(g):
         ref = kv[g].at[pl.ds(0, 6)]
@@ -265,32 +267,36 @@
         valid, slot = picks(h)
         top = None
         for t in range(TOPK + 1):
-            s = lax.dot_general(q, kv[2 * h][slot[t]], (((1,), (1,)), ((), ())),
+            s = lax.dot_general(kv[2 * h][slot[t]], q, (((1,), (1,)), ((), ())),
                                 preferred_element_type=jnp.float32)
             if t == 0:
                 s = jnp.where(token + c * TOK >= key_at, s, NEG)
             scores[t] = s
-            high = jnp.max(s, axis=1, keepdims=True)
+            high = jnp.max(s, axis=0, keepdims=True)
             top = high if t == 0 else jnp.maximum(top, jnp.where(valid[t], high, NEG))
         total = None
         for t in range(TOPK + 1):
             shift = top if t == 0 else jnp.where(valid[t], top, -NEG)
             p = jnp.exp2((scores[t] - shift) * RATE)
-            add = jnp.sum(p, axis=1, keepdims=True)
+            add = jnp.sum(p, axis=0, keepdims=True)
             weights[c, t] = p.astype(jnp.bfloat16)
             total = add if t == 0 else total + add
-        totals[c] = jnp.broadcast_to(total, (GRP * TOK, DH))
+        totals[c] = jnp.broadcast_to(total, (8, GRP * TOK))
+
+    def flip(h):
+        _, slot = picks(h)
+        for t in range(TOPK + 1):
+            flipped[t] = kv[2 * h + 1][slot[t]].T
 
     def attend(h, c, o):
-        _, slot = picks(h)
         acc = None
         for t in range(TOPK + 1):
-            part = lax.dot_general(weights[c, t], kv[2 * h + 1][slot[t]], (((1,), (0,)), ((), ())),
+            part = lax.dot_general(flipped[t], weights[c, t], (((1,), (0,)), ((), ())),
                                    preferred_element_type=jnp.float32)
             acc = part if t == 0 else acc + part
-        res = (acc / totals[c]).astype(jnp.bfloat16)
+        res = acc / totals[c, 0:1]
         for g in range(GRP):
-            obuf[h, c, :, g * DH:(g + 1) * DH] = res[g * TOK:(g + 1) * TOK]
+            obuf[h, c, :, g * DH:(g + 1) * DH] = res[:, g * TOK:(g + 1) * TOK].T.astype(jnp.bfloat16)
         for k in (1, 2, 3):
             pl.when(o == k)(lambda: out_copy(k, h).start())
         pl.when(o == 0)(lambda: out_local(h).start())
@@ -313,6 +319,7 @@
 
     def attend_phase(h, steps):
         whole(2 * h + 1).wait_recv()
+        flip(h)
         phase(h, attend, steps)
 
     weigh_phase(0, [(0, done + 1), (2, done + 2)])
@@ -341,15 +348,16 @@
 
     return pl.pallas_call(
         body,
-        out_shape=jax.ShapeDtypeStruct(query.shape, jnp.bfloat16),
+        out_shape=pltpu.VMEM(query.shape, jnp.bfloat16),
         in_specs=[pl.BlockSpec(memory_space=pltpu.SMEM), any_spec, any_spec, any_spec],
-        out_specs=any_spec,
+        out_specs=pl.BlockSpec(memory_space=pltpu.VMEM),
         scratch_shapes=[pltpu.VMEM((SLOTS, BLK, DH), jnp.bfloat16)] * GROUPS + [
             pltpu.VMEM((HLOC, NHEAD, TOK, WIDE), jnp.bfloat16),
             pltpu.VMEM((HLOC, NHEAD, TOK, WIDE), jnp.bfloat16),
             pltpu.VMEM((TOPK + 1, GRP * TOK, BLK), jnp.float32),
             pltpu.VMEM((NHEAD, TOPK + 1, GRP * TOK, BLK), jnp.bfloat16),
-            pltpu.VMEM((NHEAD, GRP * TOK, DH), jnp.float32),
+            pltpu.VMEM((NHEAD, 8, GRP * TOK), jnp.float32),
+            pltpu.VMEM((TOPK + 1, DH, BLK), jnp.bfloat16),
             dma((GROUPS,)), dma((GROUPS,)),
             dma((HLOC,)), dma((HLOC,)),
             dma((GROUPS,)), dma((PIECES, 6)),

time: 70.7 us -> 69.2 us (0.979)
  local copies, waits for them, and re-layouts: 2.29 us -> 0.97 us
    unnamed x1, local copies, waits for them, and re-layouts: 2.29 us -> 0.97 us
where the time goes in v3:
time: 69.2 us
  Pallas kernels  68.2 us (99%)
  local copies, waits for them, and re-layouts  0.97 us (1%)
    pallas_call x1, Pallas kernels, on_device(): pl.pallas_call(body, out_shape=pltpu.VMEM(query.shape, jnp.bfloat16), in_...  68.2 us

profile of v3, /device:TPU:1, one launch (start us, length us, event | category | flops | bytes accessed | tf_op | source)
XLA Modules:
  0.0 69.2 jit_solution(7360078399600173355)
XLA Ops:
  0.0 68.2 %window_attention.1 = bf16[128,4096]{1,0:T(8,128)(2,1)S(1)} custom-call(s32[1,2,3]{2,1,0:T(2,128)} %refs_0_.1, bf16[128,4096]{1,0:T(8,128)(2,1)} %refs_1_.1, bf16[128,1024]{1,0:T(8,128)(2,1)} %refs_2_.1, bf16[128,1024]{1,0:T(8,128)(2,1)} %refs_3_.1), custom_call_target="tpu_custom_call" | custom-call | flops 4294967296 | bytes 4194304 | tf_op jit(solution)/shard_map/window_attention/pallas_call | solution.py:349
  68.2 1.0 %copy.6 = bf16[128,4096]{1,0:T(8,128)(2,1)} copy(bf16[128,4096]{1,0:T(8,128)(2,1)S(1)} %window_attention.1) | data formatting | bytes 2097152

commit v4 on v3

--- a/solution.py
+++ b/solution.py
@@ -23,12 +23,14 @@
 PIECES = GROUPS * PARTS
 ROWS = BLK // PARTS
 WIDE = GRP * DH
+BAND = 256
+BANDS = (TOPK + 1) * BLK // BAND
 NEG = -1e30
 RATE = math.log2(math.e) / math.sqrt(DH)
 MESH = pl.DeviceIdType.MESH
 
 
-def kernel(nseq, chosen, query, keys, values, out, kv0, kv1, kv2, kv3, qbuf, obuf, scores, weights, totals, flipped,
+def kernel(nseq, chosen, query, keys, values, out, kv0, kv1, kv2, kv3, qbuf, obuf, scores_a, scores_b, weights_a, weights_b, totals, flipped,
            own_send, own_recv, q_send, q_recv, win_send, win_recv, sib_send, sib_recv,
            out_send, out_recv, local_sem):
     kv = (kv0, kv1, kv2, kv3)
@@ -173,6 +175,8 @@
         @pl.when(x == 0)
         def _():
             arrived(m, 1)
+            if m // PARTS == GROUPS - 1:
+                forward(m, up, 1, 5)
             share(m, 1)
 
         @pl.when(x < 3)
@@ -213,14 +217,24 @@
             arrived(m, 6)
             share(m, 6)
 
+        if m // PARTS == GROUPS - 1:
+            @pl.when(x == 0)
+            def _():
+                arrived(m, 5)
+                share(m, 5)
+
     def lag4(m):
         @pl.when(x < 2)
         def _():
             arrived(m, 6)
-            when(x == 1, m, left, 6, 5)
+            if m // PARTS < GROUPS - 1:
+                when(x == 1, m, left, 6, 5)
             share(m, 6)
 
     def lag5(m):
+        if m // PARTS == GROUPS - 1:
+            return
+
         @pl.when(x == 0)
         def _():
             arrived(m, 5)
@@ -246,92 +260,139 @@
         if n == 4:
             send_q(1)
 
-    key_at = lax.broadcasted_iota(jnp.int32, (BLK, GRP * TOK), 0)
-    token = lax.rem(lax.broadcasted_iota(jnp.int32, (BLK, GRP * TOK), 1), TOK)
-
-    def whole(g):
-        ref = kv[g].at[pl.ds(0, 6)]
+    def whole(g, slots=6):
+        ref = kv[g].at[pl.ds(0, slots)]
         return remote(ref, ref, sib_send.at[g], sib_recv.at[g], sibling)
+
+    def chunk(j):
+        return lax.rem(y + j + 1, NHEAD)
 
     def picks(h):
         valid, slot = [None], [0]
         for t in range(TOPK):
-            pick = chosen[0, h, t]
-            valid.append(pick >= 0)
-            slot.append(jnp.where(pick >= 0, jnp.clip(seq - pick, 0, SLOTS - 1), 0))
+            named = chosen[0, h, t]
+            valid.append(named >= 0)
+            slot.append(jnp.where(named >= 0, jnp.clip(seq - named, 0, SLOTS - 1), 0))
         return valid, slot
 
-    def weigh(h, c):
+    behind = (lax.broadcasted_iota(jnp.int32, (BAND, TOK), 0)
+              - lax.broadcasted_iota(jnp.int32, (BAND, TOK), 1))
+    weights = (weights_a, weights_b)
+
+    def queries(h, c):
         wide = qbuf[h, c]
-        q = jnp.concatenate([wide[:, g * DH:(g + 1) * DH] for g in range(GRP)], axis=0)
+        return jnp.concatenate([wide[:, g * DH:(g + 1) * DH] for g in range(GRP)], axis=0)
+
+    def multiply(h, c, q, u, into, top):
         valid, slot = picks(h)
-        top = None
-        for t in range(TOPK + 1):
-            s = lax.dot_general(kv[2 * h][slot[t]], q, (((1,), (1,)), ((), ())),
-                                preferred_element_type=jnp.float32)
-            if t == 0:
-                s = jnp.where(token + c * TOK >= key_at, s, NEG)
-            scores[t] = s
-            high = jnp.max(s, axis=0, keepdims=True)
-            top = high if t == 0 else jnp.maximum(top, jnp.where(valid[t], high, NEG))
-        total = None
-        for t in range(TOPK + 1):
-            shift = top if t == 0 else jnp.where(valid[t], top, -NEG)
-            p = jnp.exp2((scores[t] - shift) * RATE)
-            add = jnp.sum(p, axis=0, keepdims=True)
-            weights[c, t] = p.astype(jnp.bfloat16)
-            total = add if t == 0 else total + add
-        totals[c] = jnp.broadcast_to(total, (8, GRP * TOK))
+        t, half = u // 2, u % 2
+        s = lax.dot_general(kv[2 * h][slot[t], half * BAND:(half + 1) * BAND], q, (((1,), (1,)), ((), ())),
+                            preferred_element_type=jnp.float32)
+        if t == 0:
+            seen = behind <= c * TOK - u * BAND
+            s = jnp.concatenate(
+                [jnp.where(seen, s[:, g * TOK:(g + 1) * TOK], NEG) for g in range(GRP)], axis=1)
+        into[u] = s
+        high = jnp.max(s, axis=0, keepdims=True)
+        if t > 0:
+            high = jnp.where(valid[t], high, NEG)
+        return high if top is None else jnp.maximum(top, high)
+
+    def exponent(h, c, u, source, top, total):
+        valid, _ = picks(h)
+        shift = top if u < 2 else jnp.where(valid[u // 2], top, -NEG)
+        p = jnp.exp2((source[u] - shift) * RATE)
+        weights[h][c, u * BAND:(u + 1) * BAND] = p.astype(jnp.bfloat16)
+        add = jnp.sum(p, axis=0, keepdims=True)
+        return add if total is None else total + add
 
     def flip(h):
         _, slot = picks(h)
         for t in range(TOPK + 1):
-            flipped[t] = kv[2 * h + 1][slot[t]].T
-
-    def attend(h, c, o):
-        acc = None
-        for t in range(TOPK + 1):
-            part = lax.dot_general(flipped[t], weights[c, t], (((1,), (0,)), ((), ())),
-                                   preferred_element_type=jnp.float32)
-            acc = part if t == 0 else acc + part
-        res = acc / totals[c, 0:1]
-        for g in range(GRP):
-            obuf[h, c, :, g * DH:(g + 1) * DH] = res[:, g * TOK:(g + 1) * TOK].T.astype(jnp.bfloat16)
+            flipped[h, :, t * BLK:(t + 1) * BLK] = kv[2 * h + 1][slot[t]].T
+
+    def attend(h, c, side):
+        q0 = side * 2 * TOK
+        acc = lax.dot_general(flipped[h], weights[h][c, :, q0:q0 + 2 * TOK], (((1,), (0,)), ((), ())),
+                              preferred_element_type=jnp.float32)
+        res = acc / totals[h, c, 0:1, q0:q0 + 2 * TOK]
+        for g in range(2):
+            obuf[h, c, :, q0 + g * DH:q0 + (g + 1) * DH] = res[:, g * TOK:(g + 1) * TOK].T.astype(jnp.bfloat16)
+
+    def hand_out(h, j):
+        o = lax.rem(j + 1, NHEAD)
         for k in (1, 2, 3):
             pl.when(o == k)(lambda: out_copy(k, h).start())
         pl.when(o == 0)(lambda: out_local(h).start())
 
-    def phase(h, work, steps):
-        def body(j, _):
-            o = lax.rem(j + 1, NHEAD)
-            work(h, lax.rem(y + o, NHEAD), o)
-            for after, n in steps:
-                pl.when(j == after)(lambda: step(n))
-            return 0
-
-        lax.fori_loop(0, NHEAD, body, 0)
-
-    def weigh_phase(h, steps):
+    def weigh(h, j, source, top, into, other):
+        c, later = chunk(j), chunk(j + 1)
+        q = queries(h, later)
+        total, ahead = None, None
+        for u in range(BANDS):
+            ahead = multiply(h, later, q, u, into, ahead)
+            total = exponent(h, c, u, source, top, total)
+            if other is not None and u % 4 == 3:
+                attend(other, c, u // 4)
+        totals[h, c] = jnp.broadcast_to(total, (8, GRP * TOK))
+        return ahead
+
+    def weigh_phase(h, other, steps):
         whole(2 * h).wait_recv()
         q_three(h).wait_recv()
         q_local(h).wait()
-        phase(h, lambda h, c, o: weigh(h, c), steps)
-
-    def attend_phase(h, steps):
-        whole(2 * h + 1).wait_recv()
-        flip(h)
-        phase(h, attend, steps)
-
-    weigh_phase(0, [(0, done + 1), (2, done + 2)])
-    attend_phase(0, [(1, done + 3), (3, done + 4)])
-    weigh_phase(1, [(0, done + 5), (2, done + 6)])
-    attend_phase(1, [])
+        if other is not None:
+            whole(2 * other + 1).wait_recv()
+            flip(other)
+        q = queries(h, chunk(0))
+        top = None
+        for u in range(BANDS):
+            top = multiply(h, chunk(0), q, u, scores_a, top)
+
+        def after(jj, place):
+            if other is not None:
+                hand_out(other, 2 * jj + place)
+            for at_jj, at_place, n in steps:
+                if at_place == place:
+                    pl.when(jj == at_jj)(lambda: step(n))
+
+        def body(jj, top):
+            top = weigh(h, 2 * jj, scores_a, top, scores_b, other)
+            after(jj, 0)
+            top = weigh(h, 2 * jj + 1, scores_b, top, scores_a, other)
+            after(jj, 1)
+            return top
+
+        lax.fori_loop(0, NHEAD // 2, body, top)
+
+    weigh_phase(0, None, [(0, 0, done + 1), (0, 1, done + 2), (1, 0, done + 3), (1, 1, done + 4)])
+    weigh_phase(1, 0, [(0, 0, done + 5)])
+
+    whole(2 * HLOC - 1).wait_recv()
+    flip(HLOC - 1)
+
+    def finish(j, _):
+        for side in range(2):
+            attend(HLOC - 1, chunk(j), side)
+        hand_out(HLOC - 1, j)
+        return 0
+
+    lax.fori_loop(0, NHEAD, finish, 0)
 
     for g in range(GROUPS):
         kv_three(g).wait_send()
         whole(g).wait_send()
-        ref = kv[g].at[pl.ds(0, 6)]
-        remote(ref, ref, win_send.at[g], sib_recv.at[g], up).wait_send()
+
+        def sent(slots):
+            ref = kv[g].at[pl.ds(0, slots)]
+            remote(ref, ref, win_send.at[g], sib_recv.at[g], up).wait_send()
+
+        if g < GROUPS - 1:
+            sent(6)
+        else:
+            pl.when(x == 0)(lambda: sent(7))
+            pl.when(x == 1)(lambda: sent(5))
+            pl.when(x > 1)(lambda: sent(6))
     for h in range(HLOC):
         q_three(h).wait_send()
         out_three(h).wait()
@@ -354,10 +415,12 @@
         scratch_shapes=[pltpu.VMEM((SLOTS, BLK, DH), jnp.bfloat16)] * GROUPS + [
             pltpu.VMEM((HLOC, NHEAD, TOK, WIDE), jnp.bfloat16),
             pltpu.VMEM((HLOC, NHEAD, TOK, WIDE), jnp.bfloat16),
-            pltpu.VMEM((TOPK + 1, GRP * TOK, BLK), jnp.float32),
-            pltpu.VMEM((NHEAD, TOPK + 1, GRP * TOK, BLK), jnp.bfloat16),
-            pltpu.VMEM((NHEAD, 8, GRP * TOK), jnp.float32),
-            pltpu.VMEM((TOPK + 1, DH, BLK), jnp.bfloat16),
+            pltpu.VMEM((BANDS, BAND, GRP * TOK), jnp.float32),
+            pltpu.VMEM((BANDS, BAND, GRP * TOK), jnp.float32),
+            pltpu.VMEM((NHEAD, (TOPK + 1) * BLK, GRP * TOK), jnp.bfloat16),
+            pltpu.VMEM((NHEAD, (TOPK + 1) * BLK, GRP * TOK), jnp.bfloat16),
+            pltpu.VMEM((HLOC, NHEAD, 8, GRP * TOK), jnp.float32),
+            pltpu.VMEM((HLOC, DH, (TOPK + 1) * BLK), jnp.bfloat16),
             dma((GROUPS,)), dma((GROUPS,)),
             dma((HLOC,)), dma((HLOC,)),
             dma((GROUPS,)), dma((PIECES, 6)),

time: 69.2 us -> 71.8 us (1.038)
  Pallas kernels: 68.2 us -> 70.7 us
    pallas_call x1, Pallas kernels: 68.2 us -> 70.7 us  [on_device(): pl.pallas_call(body, out_shape=pltpu.VMEM(query.shape, jnp.bfloat16), in_...]
where the time goes in v4:
time: 71.8 us; the launch traced here: 71.7 us
  Pallas kernels  70.7 us (98%)
  local copies, waits for them, and re-layouts  0.97 us (1%)
    pallas_call x1, Pallas kernels, on_device(): pl.pallas_call(body, out_shape=pltpu.VMEM(query.shape, jnp.bfloat16), in_...  70.7 us

profile of v4, /device:TPU:1, one launch (start us, length us, event | category | flops | bytes accessed | tf_op | source)
XLA Modules:
  0.0 71.7 jit_solution(18272500224848048831)
XLA Ops:
  0.0 70.7 %window_attention.1 = bf16[128,4096]{1,0:T(8,128)(2,1)S(1)} custom-call(s32[1,2,3]{2,1,0:T(2,128)} %refs_0_.1, bf16[128,4096]{1,0:T(8,128)(2,1)} %refs_1_.1, bf16[128,1024]{1,0:T(8,128)(2,1)} %refs_2_.1, bf16[128,1024]{1,0:T(8,128)(2,1)} %refs_3_.1), custom_call_target="tpu_custom_call" | custom-call | flops 4294967296 | bytes 4194304 | tf_op jit(solution)/shard_map/window_attention/pallas_call | solution.py:410
  70.7 1.0 %copy.6 = bf16[128,4096]{1,0:T(8,128)(2,1)} copy(bf16[128,4096]{1,0:T(8,128)(2,1)S(1)} %window_attention.1) | data formatting | bytes 2097152

commit v5 on v3

--- a/solution.py
+++ b/solution.py
@@ -28,9 +28,9 @@
 MESH = pl.DeviceIdType.MESH
 
 
-def kernel(nseq, chosen, query, keys, values, out, kv0, kv1, kv2, kv3, qbuf, obuf, scores, weights, totals, flipped,
+def kernel(nseq, chosen, query, keys, values, out, kv0, kv1, kv2, kv3, qbuf, obuf, scores, weights, totals, flipped, relay,
            own_send, own_recv, q_send, q_recv, win_send, win_recv, sib_send, sib_recv,
-           out_send, out_recv, local_sem):
+           out_send, out_recv, relay_recv, relay_send, local_sem):
     kv = (kv0, kv1, kv2, kv3)
     nz = nseq // (2 * NX)
     seq = lax.axis_index("seq")
@@ -91,6 +91,23 @@
     def out_copy(o, h):
         to = partner(o)
         return remote(obuf.at[h, to[1]], out_place(y, h), out_send.at[h], out_recv.at[h], to)
+
+    def half(k):
+        return pl.ds(k * TOK // 2, TOK // 2)
+
+    def out_relay(h, k):
+        return remote(obuf.at[h, partner(2)[1], half(k)], relay.at[h, k], out_send.at[h], relay_recv.at[h, k],
+                      partner(1 + 2 * k))
+
+    def out_pass(h, k):
+        relay_in = relay.at[h, k]
+        remote(relay_in, relay_in, out_send.at[h], relay_recv.at[h, k], sibling).wait_recv()
+        origin = partner(3 - 2 * k)[1]
+        remote(relay_in, out_place(origin, h).at[half(k)], relay_send.at[h], out_recv.at[h], partner(1 + 2 * k)).start()
+
+    def pass_on(h):
+        for k in range(2):
+            out_pass(h, k)
 
     def out_local(h):
         return pltpu.make_async_copy(obuf.at[h, y], out_place(y, h), local_sem.at[GROUPS + HLOC + h])
@@ -233,17 +250,25 @@
             if 0 <= n - lag < PIECES:
                 event(n - lag)
 
-    for g in range(GROUPS):
+    def send_kv(g):
         for o in (2, 1, 3):
             kv_copy(o, g).start()
         kv_local(g).start()
 
+    send_kv(0)
+
     done = PARTS - 1 + len(lags) - 1
     for n in range(done + 1):
         step(n)
+        if n == 0:
+            send_kv(1)
         if n == 1:
             send_q(0)
-        if n == 4:
+        if n == 2:
+            send_kv(2)
+        if n == 3:
+            send_kv(3)
+        if n == 5:
             send_q(1)
 
     key_at = lax.broadcasted_iota(jnp.int32, (BLK, GRP * TOK), 0)
@@ -297,16 +322,22 @@
         res = acc / totals[c, 0:1]
         for g in range(GRP):
             obuf[h, c, :, g * DH:(g + 1) * DH] = res[:, g * TOK:(g + 1) * TOK].T.astype(jnp.bfloat16)
-        for k in (1, 2, 3):
+        for k in (1, 3):
             pl.when(o == k)(lambda: out_copy(k, h).start())
+
+        @pl.when(o == 2)
+        def _():
+            for k in range(2):
+                out_relay(h, k).start()
+
         pl.when(o == 0)(lambda: out_local(h).start())
 
     def phase(h, work, steps):
         def body(j, _):
-            o = lax.rem(j + 1, NHEAD)
+            o = lax.rem(2 + 3 * j + 3 * (j // 2) + 2 * (j // 3), NHEAD)
             work(h, lax.rem(y + o, NHEAD), o)
-            for after, n in steps:
-                pl.when(j == after)(lambda: step(n))
+            for after, then in steps:
+                pl.when(j == after)(then)
             return 0
 
         lax.fori_loop(0, NHEAD, body, 0)
@@ -322,10 +353,10 @@
         flip(h)
         phase(h, attend, steps)
 
-    weigh_phase(0, [(0, done + 1), (2, done + 2)])
-    attend_phase(0, [(1, done + 3), (3, done + 4)])
-    weigh_phase(1, [(0, done + 5), (2, done + 6)])
-    attend_phase(1, [])
+    weigh_phase(0, [(0, lambda: step(done + 1)), (2, lambda: step(done + 2))])
+    attend_phase(0, [(1, lambda: step(done + 3)), (3, lambda: step(done + 4))])
+    weigh_phase(1, [(0, lambda: step(done + 5)), (1, lambda: pass_on(0)), (2, lambda: step(done + 6))])
+    attend_phase(1, [(2, lambda: pass_on(1))])
 
     for g in range(GROUPS):
         kv_three(g).wait_send()
@@ -336,6 +367,7 @@
         q_three(h).wait_send()
         out_three(h).wait()
         out_local(h).wait()
+        three(relay.at[h], relay_send.at[h], out_recv.at[h]).wait_send()
 
 
 def on_device(query, keys, values, chosen):
@@ -358,11 +390,13 @@
             pltpu.VMEM((NHEAD, TOPK + 1, GRP * TOK, BLK), jnp.bfloat16),
             pltpu.VMEM((NHEAD, 8, GRP * TOK), jnp.float32),
             pltpu.VMEM((TOPK + 1, DH, BLK), jnp.bfloat16),
+            pltpu.VMEM((HLOC, 2, TOK // 2, WIDE), jnp.bfloat16),
             dma((GROUPS,)), dma((GROUPS,)),
             dma((HLOC,)), dma((HLOC,)),
             dma((GROUPS,)), dma((PIECES, 6)),
             dma((GROUPS,)), dma((GROUPS,)),
             dma((HLOC,)), dma((HLOC,)),
+            dma((HLOC, 2)), dma((HLOC,)),
             dma((GROUPS + 2 * HLOC,)),
         ],
         compiler_params=pltpu.CompilerParams(

time: 69.2 us -> 69.8 us (level)
  no operation moved by 1% of the time
where the time goes in v5:
time: 69.8 us; the launch traced here: 69.7 us
  Pallas kernels  68.8 us (99%)
  local copies, waits for them, and re-layouts  0.97 us (1%)
    pallas_call x1, Pallas kernels, on_device(): pl.pallas_call(body, out_shape=pltpu.VMEM(query.shape, jnp.bfloat16), in_...  68.8 us

profile of v5, /device:TPU:1, one launch (start us, length us, event | category | flops | bytes accessed | tf_op | source)
XLA Modules:
  0.0 69.7 jit_solution(1910958392261544589)
XLA Ops:
  0.0 68.8 %window_attention.1 = bf16[128,4096]{1,0:T(8,128)(2,1)S(1)} custom-call(s32[1,2,3]{2,1,0:T(2,128)} %refs_0_.1, bf16[128,4096]{1,0:T(8,128)(2,1)} %refs_1_.1, bf16[128,1024]{1,0:T(8,128)(2,1)} %refs_2_.1, bf16[128,1024]{1,0:T(8,128)(2,1)} %refs_3_.1), custom_call_target="tpu_custom_call" | custom-call | flops 4294967296 | bytes 4194304 | tf_op jit(solution)/shard_map/window_attention/pallas_call | solution.py:381
  68.8 1.0 %copy.6 = bf16[128,4096]{1,0:T(8,128)(2,1)} copy(bf16[128,4096]{1,0:T(8,128)(2,1)S(1)} %window_attention.1) | data formatting | bytes 2097152

commit v6 on v3

v6 whole, which is shorter than its diff:
```python
import math

import jax
import jax.numpy as jnp
from jax import lax
from jax.experimental import pallas as pl
from jax.experimental.pallas import tpu as pltpu
from jax.sharding import PartitionSpec as P

HQ = 32
HK = 8
DH = 128
BLK = 512
TOPK = 3
GRP = HQ // HK
NHEAD = 4
HLOC = HK // NHEAD
TOK = BLK // NHEAD
NX = 4
SLOTS = 13
GROUPS = 2 * HLOC
PARTS = 2
PIECES = GROUPS * PARTS
ROWS = BLK // PARTS
WIDE = GRP * DH
NEG = -1e30
RATE = math.log2(math.e) / math.sqrt(DH)
MESH = pl.DeviceIdType.MESH

ROUTES = {
    0: [
        (0, 0), (0, "Z", 0, 4), (0, "P", 0, 1), (0, "M", 0, 3), (2, 4),
        (2, "P", 4, 5), (4, 1), (4, "Z", 1, 5, 6, 8), (4, 3), (4, "M", 3, 6), (6, 2),
        (6, "Z", 2, 6), (9, 6), (10, 5),
    ],
    1: [
        (0, 0), (0, "Z", 0, 4), (0, "P", 0, 1), (2, 4), (2, "M", 4, 3),
        (2, "P", 4, 5), (2, 1), (4, 3), (4, 5), (6, 2),
        (6, "Z", 2, 6), (8, 6), (8, "M", 6, 5, 0, 6),
    ],
    2: [
        (0, 0), (0, "Z", 0, 4), (0, "P", 0, 1), (2, 4), (2, "M", 4, 3),
        (2, 1), (2, "P", 1, 2), (4, 3), (4, "M", 3, 2), (4, 2),
        (4, "Z", 2, 6), (4, 5), (6, 6),
    ],
    3: [
        (0, 0), (0, "Z", 0, 4), (2, 4), (2, "P", 4, 1), (2, "M", 4, 3),
        (2, 3), (2, "M", 3, 2), (2, 1), (2, "Z", 1, 5), (4, 5),
        (4, "P", 5, 2), (4, 2), (5, 6),
    ],
}
TICKS = 18
ITEM_TICKS = (12, 12, 13, 14, 14, 14, 15, 16, 16, 16, 17, 17, 17, 17, 17, 17)


def kernel(nseq, chosen, query, keys, values, out, kv, blocks, qbuf, obuf, scores, weights, totals, flipped,
           own_send, own_recv, q_send, q_recv, win_send, win_recv, sib_send, sib_recv,
           out_send, out_recv, local_sem):
    nz = nseq // (2 * NX)
    seq = lax.axis_index("seq")
    y = lax.axis_index("head")
    core = lax.rem(seq, 2)
    x = lax.rem(seq // 2, NX)
    z = seq // (2 * NX)

    def at(zz, xx):
        return ((zz * NX + xx) * 2 + core, y)

    up = at(lax.rem(z + 1, nz), x)
    down = at(lax.rem(z + nz - 1, nz), x)
    right = at(z, lax.rem(x + 1, NX))
    left = at(z, lax.rem(x + NX - 1, NX))
    sibling = (seq + 1 - 2 * core, y)

    def partner(o):
        return (seq, lax.rem(y + o, NHEAD))

    place = z * NX + x
    barrier = pltpu.get_barrier_semaphore()

    def greet(who):
        pl.semaphore_signal(barrier, inc=1, device_id=who, device_id_type=MESH)

    for who in [right, left, sibling, partner(1), partner(2), partner(3)]:
        greet(who)
    pl.when(z < nz - 1)(lambda: greet(up))
    pl.when(z > 0)(lambda: greet(down))
    edge = (z == 0) | (z == nz - 1)
    pl.when(edge)(lambda: pl.semaphore_wait(barrier, 7))
    pl.when(jnp.logical_not(edge))(lambda: pl.semaphore_wait(barrier, 8))

    def columns(start, width):
        return pl.ds(pl.multiple_of(start, DH), width)

    def remote(src, dst, send, recv, to):
        return pltpu.make_async_remote_copy(
            src_ref=src, dst_ref=dst, send_sem=send, recv_sem=recv, device_id=to, device_id_type=MESH)

    own_rows = pl.ds(pl.multiple_of(y * TOK, TOK), TOK)

    def kv_source(h, i, to_y):
        return (keys, values)[i].at[:, columns((to_y * HLOC + h) * DH, DH)]

    def kv_copy(o, h, i):
        to, g = partner(o), 2 * h + i
        return remote(kv_source(h, i, to[1]), kv.at[g, 0, own_rows], own_send.at[g], own_recv.at[g], to)

    def kv_local(h, i):
        return pltpu.make_async_copy(kv_source(h, i, y), kv.at[2 * h + i, 0, own_rows], local_sem.at[2 * h + i])

    def q_source(h, to_y):
        return query.at[:, columns((to_y * HLOC + h) * WIDE, WIDE)]

    def q_copy(o, h):
        to = partner(o)
        return remote(q_source(h, to[1]), qbuf.at[h, y], q_send.at[h], q_recv.at[h], to)

    def q_local(h):
        return pltpu.make_async_copy(q_source(h, y), qbuf.at[h, y], local_sem.at[GROUPS + h])

    def q_local_wait(h):
        pltpu.make_async_copy(qbuf.at[h, 0], qbuf.at[h, 0], local_sem.at[GROUPS + h]).wait()

    def out_place(to_y, h):
        return out.at[:, columns((to_y * HLOC + h) * WIDE, WIDE)]

    def out_copy(o, h):
        to = partner(o)
        return remote(obuf.at[h, to[1]], out_place(y, h), out_send.at[h], out_recv.at[h], to)

    def out_local(h):
        return pltpu.make_async_copy(obuf.at[h, y], out_place(y, h), local_sem.at[GROUPS + HLOC + h])

    def three(ref, send, recv):
        return remote(ref, ref, send, recv, sibling)

    def kv_three(g):
        return three(kv.at[g, 0, pl.ds(0, 3 * TOK)], own_send.at[g], own_recv.at[g])

    def kv_local_wait(g):
        ref = kv.at[g, 0, pl.ds(0, TOK)]
        pltpu.make_async_copy(ref, ref, local_sem.at[g]).wait()

    def q_three(h):
        return three(qbuf.at[h, pl.ds(0, 3)], q_send.at[h], q_recv.at[h])

    def out_three(h):
        return three(obuf.at[h, pl.ds(0, 3)], out_send.at[h], out_recv.at[h])

    def send_q(h):
        for o in (2, 1, 3):
            q_copy(o, h).start()
        q_local(h).start()

    def piece(m, slot):
        return kv.at[m // PARTS, slot, pl.ds(pl.multiple_of(lax.rem(m, PARTS) * ROWS, ROWS), ROWS)]

    def forward(m, to, r, into):
        remote(piece(m, 2 * r), piece(m, 2 * into),
               win_send.at[m // PARTS], win_recv.at[m, into - 1], to).start()

    def arrived(m, r):
        remote(piece(m, 2 * r), piece(m, 2 * r), win_send.at[m // PARTS], win_recv.at[m, r - 1], up).wait_recv()

    def share(m, r):
        g = m // PARTS

        def go():
            remote(kv.at[g, 2 * r], kv.at[g, 2 * r + 1 - 2 * core], sib_send.at[g], sib_recv.at[g], sibling).start()

        whole_slot = lax.rem(m, PARTS) == PARTS - 1
        if r == 0:
            whole_slot = whole_slot & (core == 0)
        elif r == 6:
            whole_slot = whole_slot & (core == 1)
        pl.when(whole_slot)(go)

    def own(m):
        @pl.when(lax.rem(m, PARTS) == 0)
        def _():
            kv_three(m // PARTS).wait_recv()
            kv_local_wait(m // PARTS)

    def event(m, entry):
        if len(entry) > 2:
            there = place >= entry[2]
            if entry[1] == "Z":
                there = there & (z < nz - 1)
            if len(entry) > 4:
                there = there & (m >= entry[4]) & (m < entry[5])
            to = {"Z": up, "P": right, "M": left}[entry[1]]
            pl.when(there)(lambda: forward(m, to, entry[2], entry[3]))
        else:
            if entry[1] == 0:
                own(m)
            else:
                pl.when(place >= entry[1])(lambda: arrived(m, entry[1]))
            share(m, entry[1])

    def step(n):
        for xx in range(NX):
            @pl.when(x == xx)
            def _():
                for lag in sorted({entry[0] for entry in ROUTES[xx]}):
                    m = n - lag

                    @pl.when((m >= 0) & (m < PIECES))
                    def _():
                        for entry in ROUTES[xx]:
                            if entry[0] == lag:
                                event(m, entry)

    def send_kv(h, _):
        for i in range(2):
            for o in (2, 1, 3):
                kv_copy(o, h, i).start()
            kv_local(h, i).start()
        return 0

    lax.fori_loop(0, HLOC, send_kv, 0)

    def whole(g, slots=6):
        ref = kv.at[g, pl.ds(0, slots)]
        return remote(ref, ref, sib_send.at[g], sib_recv.at[g], sibling)

    def picks(h):
        valid, slot = [None], [0]
        for t in range(TOPK):
            pick = chosen[0, h, t]
            valid.append(pick >= 0)
            slot.append(seq - pick)
        return valid, slot

    def collect(g):
        _, slot = picks(g // 2)

        def part(i, _):
            rows = pl.ds(pl.multiple_of(i * DH, DH), DH)
            block = kv[g, 0, rows]
            blocks[g % 2, 0, rows] = block
            found = [block] * TOPK
            for d in range(1, SLOTS):
                block = kv[g, d, rows]
                for t in range(TOPK):
                    found[t] = jnp.where(slot[t + 1] == d, block, found[t])
            for t in range(TOPK):
                blocks[g % 2, t + 1, rows] = found[t]
            return 0

        lax.fori_loop(0, BLK // DH, part, 0)

    behind = (lax.broadcasted_iota(jnp.int32, (BLK, TOK), 0)
              - lax.broadcasted_iota(jnp.int32, (BLK, TOK), 1))

    def weigh(h, j):
        @pl.when(j == 0)
        def _():
            whole(2 * h).wait_recv()
            q_three(h).wait_recv()
            q_local_wait(h)
            collect(2 * h)

        c = lax.rem(y + j + 1, NHEAD)
        wide = qbuf[h, c]
        q = jnp.concatenate([wide[:, g * DH:(g + 1) * DH] for g in range(GRP)], axis=0)
        valid, _ = picks(h)
        top = None
        for t in range(TOPK + 1):
            s = lax.dot_general(blocks[0, t], q, (((1,), (1,)), ((), ())), preferred_element_type=jnp.float32)
            if t == 0:
                seen = behind <= c * TOK
                s = jnp.concatenate(
                    [jnp.where(seen, s[:, g * TOK:(g + 1) * TOK], NEG) for g in range(GRP)], axis=1)
            scores[t] = s
            high = jnp.max(s, axis=0, keepdims=True)
            top = high if t == 0 else jnp.maximum(top, jnp.where(valid[t], high, NEG))
        total = None
        for t in range(TOPK + 1):
            shift = top if t == 0 else jnp.where(valid[t], top, -NEG)
            p = jnp.exp2((scores[t] - shift) * RATE)
            add = jnp.sum(p, axis=0, keepdims=True)
            weights[c, t] = p.astype(jnp.bfloat16)
            total = add if t == 0 else total + add
        totals[c] = jnp.broadcast_to(total, (8, GRP * TOK))

    def attend(h, j):
        @pl.when(j == 0)
        def _():
            whole(2 * h + 1).wait_recv()
            collect(2 * h + 1)
            for t in range(TOPK + 1):
                flipped[t] = blocks[1, t].T

        o = lax.rem(j + 1, NHEAD)
        c = lax.rem(y + o, NHEAD)
        acc = None
        for t in range(TOPK + 1):
            part = lax.dot_general(flipped[t], weights[c, t], (((1,), (0,)), ((), ())),
                                   preferred_element_type=jnp.float32)
            acc = part if t == 0 else acc + part
        res = acc / totals[c, 0:1]
        for g in range(GRP):
            obuf[h, c, :, g * DH:(g + 1) * DH] = res[:, g * TOK:(g + 1) * TOK].T.astype(jnp.bfloat16)
        for k in (1, 2, 3):
            pl.when(o == k)(lambda: out_copy(k, h).start())
        pl.when(o == 0)(lambda: out_local(h).start())

    def before(n):
        return sum((n + 63 - tick) // 64 for tick in ITEM_TICKS)

    def item(k, _):
        h, kind, j = k // 8, lax.rem(k // 4, 2), lax.rem(k, 4)
        pl.when(kind == 0)(lambda: weigh(h, j))
        pl.when(kind == 1)(lambda: attend(h, j))
        return 0

    def tick(n, _):
        step(n)
        pl.when((n == 3) | (n == 6))(lambda: send_q(n // 6))
        lax.fori_loop(before(n), before(n + 1), item, 0)
        return 0

    lax.fori_loop(0, TICKS, tick, 0)

    def sent(g, m):
        for xx in range(NX):
            for low, high in ((0, 1), (1, 2), (2, nz - 1), (nz - 1, nz)):
                count = 0
                for entry in ROUTES[xx]:
                    if len(entry) > 2 and low * NX + xx >= entry[2] and (entry[1] != "Z" or low < nz - 1):
                        count += len(entry) == 4 or entry[4] <= m < entry[5]
                if count == 0:
                    continue

                @pl.when((x == xx) & (z >= low) & (z < high))
                def _():
                    ref = kv.at[g, pl.ds(0, count)]
                    remote(ref, ref, win_send.at[g], sib_recv.at[g], right).wait_send()

    def finish(g, _):
        kv_three(g).wait_send()
        whole(g).wait_send()
        pl.when(g < GROUPS - 1)(lambda: sent(g, 0))
        pl.when(g == GROUPS - 1)(lambda: sent(g, PIECES - 1))
        return 0

    lax.fori_loop(0, GROUPS, finish, 0)
    for h in range(HLOC):
        q_three(h).wait_send()
        out_three(h).wait()
        out_local(h).wait()


def on_device(query, keys, values, chosen):
    nseq = lax.axis_size("seq")
    dma = pltpu.SemaphoreType.DMA
    any_spec = pl.BlockSpec(memory_space=pl.ANY)

    def body(*refs):
        kernel(nseq, *refs)

    return pl.pallas_call(
        body,
        out_shape=pltpu.VMEM(query.shape, jnp.bfloat16),
        in_specs=[pl.BlockSpec(memory_space=pltpu.SMEM), any_spec, any_spec, any_spec],
        out_specs=pl.BlockSpec(memory_space=pltpu.VMEM),
        scratch_shapes=[
            pltpu.VMEM((GROUPS, SLOTS, BLK, DH), jnp.bfloat16),
            pltpu.VMEM((2, TOPK + 1, BLK, DH), jnp.bfloat16),
            pltpu.VMEM((HLOC, NHEAD, TOK, WIDE), jnp.bfloat16),
            pltpu.VMEM((HLOC, NHEAD, TOK, WIDE), jnp.bfloat16),
            pltpu.VMEM((TOPK + 1, GRP * TOK, BLK), jnp.float32),
            pltpu.VMEM((NHEAD, TOPK + 1, GRP * TOK, BLK), jnp.bfloat16),
            pltpu.VMEM((NHEAD, 8, GRP * TOK), jnp.float32),
            pltpu.VMEM((TOPK + 1, DH, BLK), jnp.bfloat16),
            dma((GROUPS,)), dma((GROUPS,)),
            dma((HLOC,)), dma((HLOC,)),
            dma((GROUPS,)), dma((PIECES, 6)),
            dma((GROUPS,)), dma((GROUPS,)),
            dma((HLOC,)), dma((HLOC,)),
            dma((GROUPS + 2 * HLOC,)),
        ],
        compiler_params=pltpu.CompilerParams(
            collective_id=0, has_side_effects=True, vmem_limit_bytes=56 * 1024 * 1024),
        cost_estimate=pl.CostEstimate(
            flops=4 * BLK * HLOC * GRP * BLK * 4 * DH, bytes_accessed=4 * 1024 * 1024,
            transcendentals=HLOC * GRP * BLK * BLK * 4),
        name="window_attention",
    )(chosen, query, keys, values)


def solution(mesh):
    in_specs = (
        P(("seq", "head"), None),
        P(("seq", "head"), None),
        P(("seq", "head"), None),
        P("seq", "head", None),
    )
    return jax.shard_map(
        on_device, mesh=mesh, in_specs=in_specs, out_specs=P(("seq", "head"), None), check_vma=False
    )
```

time: 69.2 us -> 65.9 us (0.952)
  the two profiles are of different devices: /device:TPU:1 before, /device:TPU:160 now
where the time goes in v6:
time: 65.9 us; the launch traced here: 65.4 us
  Pallas kernels  64.4 us (98%)
  local copies, waits for them, and re-layouts  0.97 us (1%)
    pallas_call x1, Pallas kernels, on_device(): pl.pallas_call(body, out_shape=pltpu.VMEM(query.shape, jnp.bfloat16), in_...  64.4 us

profile of v6, /device:TPU:160, one launch (start us, length us, event | category | flops | bytes accessed | tf_op | source)
XLA Modules:
  0.0 65.4 jit_solution(10079877258187567510)
XLA Ops:
  0.0 64.4 %window_attention.1 = bf16[128,4096]{1,0:T(8,128)(2,1)S(1)} custom-call(s32[1,2,3]{2,1,0:T(2,128)} %refs_0_.1, bf16[128,4096]{1,0:T(8,128)(2,1)} %refs_1_.1, bf16[128,1024]{1,0:T(8,128)(2,1)} %refs_2_.1, bf16[128,1024]{1,0:T(8,128)(2,1)} %refs_3_.1), custom_call_target="tpu_custom_call" | custom-call | flops 4294967296 | bytes 4194304 | tf_op jit(solution)/shard_map/window_attention/pallas_call | solution.py:362
  64.4 1.0 %copy.6 = bf16[128,4096]{1,0:T(8,128)(2,1)} copy(bf16[128,4096]{1,0:T(8,128)(2,1)S(1)} %window_attention.1) | data formatting | bytes 2097152

commit v7 on v6

--- a/solution.py
+++ b/solution.py
@@ -23,6 +23,7 @@
 PIECES = GROUPS * PARTS
 ROWS = BLK // PARTS
 WIDE = GRP * DH
+STRIP = 32
 NEG = -1e30
 RATE = math.log2(math.e) / math.sqrt(DH)
 MESH = pl.DeviceIdType.MESH
@@ -53,7 +54,7 @@
 ITEM_TICKS = (12, 12, 13, 14, 14, 14, 15, 16, 16, 16, 17, 17, 17, 17, 17, 17)
 
 
-def kernel(nseq, chosen, query, keys, values, out, kv, blocks, qbuf, obuf, scores, weights, totals, flipped,
+def kernel(nseq, chosen, query, keys, values, out, kv, blocks, qbuf, obuf, scores, weights, totals, flipped, turned,
            own_send, own_recv, q_send, q_recv, win_send, win_recv, sib_send, sib_recv,
            out_send, out_recv, local_sem):
     nz = nseq // (2 * NX)
@@ -249,8 +250,13 @@
 
         lax.fori_loop(0, BLK // DH, part, 0)
 
-    behind = (lax.broadcasted_iota(jnp.int32, (BLK, TOK), 0)
-              - lax.broadcasted_iota(jnp.int32, (BLK, TOK), 1))
+    behind = (lax.broadcasted_iota(jnp.int32, (TOK, TOK), 0)
+              - lax.broadcasted_iota(jnp.int32, (TOK, TOK), 1))
+
+    def fold(op, start, rows):
+        for i in range(0, rows.shape[0], 8):
+            start = op(start, rows[i:i + 8])
+        return start
 
     def weigh(h, j):
         @pl.when(j == 0)
@@ -261,27 +267,34 @@
             collect(2 * h)
 
         c = lax.rem(y + j + 1, NHEAD)
-        wide = qbuf[h, c]
-        q = jnp.concatenate([wide[:, g * DH:(g + 1) * DH] for g in range(GRP)], axis=0)
+        for g in range(GRP):
+            turned[:, g * TOK:(g + 1) * TOK] = qbuf[h, c, :, g * DH:(g + 1) * DH].T
         valid, _ = picks(h)
         top = None
         for t in range(TOPK + 1):
-            s = lax.dot_general(blocks[0, t], q, (((1,), (1,)), ((), ())), preferred_element_type=jnp.float32)
-            if t == 0:
-                seen = behind <= c * TOK
-                s = jnp.concatenate(
-                    [jnp.where(seen, s[:, g * TOK:(g + 1) * TOK], NEG) for g in range(GRP)], axis=1)
-            scores[t] = s
-            high = jnp.max(s, axis=0, keepdims=True)
+            high = jnp.full((8, GRP * TOK), NEG, jnp.float32)
+            for i in range(BLK // TOK):
+                s = jnp.dot(blocks[0, t, i * TOK:(i + 1) * TOK], turned[...], preferred_element_type=jnp.float32)
+                if t == 0:
+                    seen = behind <= (c - i) * TOK
+                    s = jnp.concatenate(
+                        [jnp.where(seen, s[:, g * TOK:(g + 1) * TOK], NEG) for g in range(GRP)], axis=1)
+                scores[t, i * TOK:(i + 1) * TOK] = s
+                high = fold(jnp.maximum, high, s)
+            high = jnp.max(high, axis=0, keepdims=True)
             top = high if t == 0 else jnp.maximum(top, jnp.where(valid[t], high, NEG))
-        total = None
+        total = jnp.zeros((8, GRP * TOK), jnp.float32)
         for t in range(TOPK + 1):
             shift = top if t == 0 else jnp.where(valid[t], top, -NEG)
-            p = jnp.exp2((scores[t] - shift) * RATE)
-            add = jnp.sum(p, axis=0, keepdims=True)
-            weights[c, t] = p.astype(jnp.bfloat16)
-            total = add if t == 0 else total + add
-        totals[c] = jnp.broadcast_to(total, (8, GRP * TOK))
+
+            def band(i, total):
+                rows = pl.ds(pl.multiple_of(i * STRIP, STRIP), STRIP)
+                p = jnp.exp2((scores[t, rows] - shift) * RATE)
+                weights[c, pl.ds(pl.multiple_of(t * BLK + i * STRIP, STRIP), STRIP)] = p.astype(jnp.bfloat16)
+                return fold(jnp.add, total, p)
+
+            total = lax.fori_loop(0, BLK // STRIP, band, total, unroll=4)
+        totals[c] = jnp.broadcast_to(jnp.sum(total, axis=0, keepdims=True), (8, GRP * TOK))
 
     def attend(h, j):
         @pl.when(j == 0)
@@ -289,18 +302,16 @@
             whole(2 * h + 1).wait_recv()
             collect(2 * h + 1)
             for t in range(TOPK + 1):
-                flipped[t] = blocks[1, t].T
+                flipped[:, t * BLK:(t + 1) * BLK] = blocks[1, t].T
 
         o = lax.rem(j + 1, NHEAD)
         c = lax.rem(y + o, NHEAD)
-        acc = None
-        for t in range(TOPK + 1):
-            part = lax.dot_general(flipped[t], weights[c, t], (((1,), (0,)), ((), ())),
-                                   preferred_element_type=jnp.float32)
-            acc = part if t == 0 else acc + part
-        res = acc / totals[c, 0:1]
-        for g in range(GRP):
-            obuf[h, c, :, g * DH:(g + 1) * DH] = res[:, g * TOK:(g + 1) * TOK].T.astype(jnp.bfloat16)
+        for side in range(2):
+            q0 = side * 2 * TOK
+            acc = jnp.dot(flipped[...], weights[c, :, q0:q0 + 2 * TOK], preferred_element_type=jnp.float32)
+            res = acc / totals[c, 0:1, q0:q0 + 2 * TOK]
+            for g in range(2):
+                obuf[h, c, :, q0 + g * DH:q0 + (g + 1) * DH] = res[:, g * TOK:(g + 1) * TOK].T.astype(jnp.bfloat16)
         for k in (1, 2, 3):
             pl.when(o == k)(lambda: out_copy(k, h).start())
         pl.when(o == 0)(lambda: out_local(h).start())
@@ -369,10 +380,11 @@
             pltpu.VMEM((2, TOPK + 1, BLK, DH), jnp.bfloat16),
             pltpu.VMEM((HLOC, NHEAD, TOK, WIDE), jnp.bfloat16),
             pltpu.VMEM((HLOC, NHEAD, TOK, WIDE), jnp.bfloat16),
-            pltpu.VMEM((TOPK + 1, GRP * TOK, BLK), jnp.float32),
-            pltpu.VMEM((NHEAD, TOPK + 1, GRP * TOK, BLK), jnp.bfloat16),
+            pltpu.VMEM((TOPK + 1, BLK, GRP * TOK), jnp.float32),
+            pltpu.VMEM((NHEAD, (TOPK + 1) * BLK, GRP * TOK), jnp.bfloat16),
             pltpu.VMEM((NHEAD, 8, GRP * TOK), jnp.float32),
-            pltpu.VMEM((TOPK + 1, DH, BLK), jnp.bfloat16),
+            pltpu.VMEM((DH, (TOPK + 1) * BLK), jnp.bfloat16),
+            pltpu.VMEM((DH, GRP * TOK), jnp.bfloat16),
             dma((GROUPS,)), dma((GROUPS,)),
             dma((HLOC,)), dma((HLOC,)),
             dma((GROUPS,)), dma((PIECES, 6)),

time: 65.9 us -> 66.2 us (level)
  no operation moved by 1% of the time
where the time goes in v7:
time: 66.2 us; the launch traced here: 65.6 us
  Pallas kernels  64.6 us (98%)
  local copies, waits for them, and re-layouts  0.97 us (1%)
    pallas_call x1, Pallas kernels, on_device(): pl.pallas_call(body, out_shape=pltpu.VMEM(query.shape, jnp.bfloat16), in_...  64.6 us

profile of v7, /device:TPU:160, one launch (start us, length us, event | category | flops | bytes accessed | tf_op | source)
XLA Modules:
  0.0 65.6 jit_solution(7793673385037041384)
XLA Ops:
  0.0 64.6 %window_attention.1 = bf16[128,4096]{1,0:T(8,128)(2,1)S(1)} custom-call(s32[1,2,3]{2,1,0:T(2,128)} %refs_0_.1, bf16[128,4096]{1,0:T(8,128)(2,1)} %refs_1_.1, bf16[128,1024]{1,0:T(8,128)(2,1)} %refs_2_.1, bf16[128,1024]{1,0:T(8,128)(2,1)} %refs_3_.1), custom_call_target="tpu_custom_call" | custom-call | flops 4294967296 | bytes 4194304 | tf_op jit(solution)/shard_map/window_attention/pallas_call | solution.py:373
  64.6 1.0 %copy.6 = bf16[128,4096]{1,0:T(8,128)(2,1)} copy(bf16[128,4096]{1,0:T(8,128)(2,1)S(1)} %window_attention.1) | data formatting | bytes 2097152

commit v8 on v7

--- a/solution.py
+++ b/solution.py
@@ -55,8 +55,9 @@
 
 
 def kernel(nseq, chosen, query, keys, values, out, kv, blocks, qbuf, obuf, scores, weights, totals, flipped, turned,
+           k_all, v_all, q_all, stage, q_relay, out_relay_buf,
            own_send, own_recv, q_send, q_recv, win_send, win_recv, sib_send, sib_recv,
-           out_send, out_recv, local_sem):
+           out_send, out_recv, q_relay_recv, q_relay_send, relay_recv, relay_send, local_sem):
     nz = nseq // (2 * NX)
     seq = lax.axis_index("seq")
     y = lax.axis_index("head")
@@ -77,6 +78,11 @@
         return (seq, lax.rem(y + o, NHEAD))
 
     place = z * NX + x
+    loads = [pltpu.make_async_copy(src, dst, local_sem.at[i])
+             for i, (src, dst) in enumerate([(keys, k_all), (values, v_all), (query, q_all)])]
+    for load in loads:
+        load.start()
+
     barrier = pltpu.get_barrier_semaphore()
 
     def greet(who):
@@ -99,23 +105,31 @@
 
     own_rows = pl.ds(pl.multiple_of(y * TOK, TOK), TOK)
 
-    def kv_source(h, i, to_y):
-        return (keys, values)[i].at[:, columns((to_y * HLOC + h) * DH, DH)]
-
-    def kv_copy(o, h, i):
-        to, g = partner(o), 2 * h + i
-        return remote(kv_source(h, i, to[1]), kv.at[g, 0, own_rows], own_send.at[g], own_recv.at[g], to)
-
-    def kv_local(h, i):
-        return pltpu.make_async_copy(kv_source(h, i, y), kv.at[2 * h + i, 0, own_rows], local_sem.at[2 * h + i])
+    def kv_copy(o, h):
+        to = partner(o)
+        return remote(stage.at[to[1] * HLOC + h], kv.at[pl.ds(2 * h, 2), 0, own_rows], own_send.at[h], own_recv.at[h], to)
+
+    def half(k):
+        return pl.ds(k * TOK // 2, TOK // 2)
 
     def q_source(h, to_y):
-        return query.at[:, columns((to_y * HLOC + h) * WIDE, WIDE)]
+        return q_all.at[:, columns((to_y * HLOC + h) * WIDE, WIDE)]
 
     def q_copy(o, h):
         to = partner(o)
         return remote(q_source(h, to[1]), qbuf.at[h, y], q_send.at[h], q_recv.at[h], to)
 
+    def q_via(h, k):
+        return remote(q_source(h, partner(2)[1]).at[half(k)], q_relay.at[h, k], q_send.at[h], q_relay_recv.at[h, k],
+                      partner(1 + 2 * k))
+
+    def q_pass(h):
+        for k in range(2):
+            ref = q_relay.at[h, k]
+            remote(ref, ref, q_send.at[h], q_relay_recv.at[h, k], sibling).wait_recv()
+            remote(ref, qbuf.at[h, partner(3 - 2 * k)[1], half(k)], q_relay_send.at[h], q_recv.at[h],
+                   partner(1 + 2 * k)).start()
+
     def q_local(h):
         return pltpu.make_async_copy(q_source(h, y), qbuf.at[h, y], local_sem.at[GROUPS + h])
 
@@ -135,12 +149,8 @@
     def three(ref, send, recv):
         return remote(ref, ref, send, recv, sibling)
 
-    def kv_three(g):
-        return three(kv.at[g, 0, pl.ds(0, 3 * TOK)], own_send.at[g], own_recv.at[g])
-
-    def kv_local_wait(g):
-        ref = kv.at[g, 0, pl.ds(0, TOK)]
-        pltpu.make_async_copy(ref, ref, local_sem.at[g]).wait()
+    def kv_three(h):
+        return three(kv.at[pl.ds(2 * h, 2), 0, pl.ds(0, 3 * TOK)], own_send.at[h], own_recv.at[h])
 
     def q_three(h):
         return three(qbuf.at[h, pl.ds(0, 3)], q_send.at[h], q_recv.at[h])
@@ -149,9 +159,22 @@
         return three(obuf.at[h, pl.ds(0, 3)], out_send.at[h], out_recv.at[h])
 
     def send_q(h):
-        for o in (2, 1, 3):
+        for k in range(2):
+            q_via(h, k).start()
+        for o in (1, 3):
             q_copy(o, h).start()
         q_local(h).start()
+
+    def out_via(h, k):
+        return remote(obuf.at[h, partner(2)[1], half(k)], out_relay_buf.at[h, k], out_send.at[h], relay_recv.at[h, k],
+                      partner(1 + 2 * k))
+
+    def out_pass(h):
+        for k in range(2):
+            ref = out_relay_buf.at[h, k]
+            remote(ref, ref, out_send.at[h], relay_recv.at[h, k], sibling).wait_recv()
+            remote(ref, out_place(partner(3 - 2 * k)[1], h).at[half(k)], relay_send.at[h], out_recv.at[h],
+                   partner(1 + 2 * k)).start()
 
     def piece(m, slot):
         return kv.at[m // PARTS, slot, pl.ds(pl.multiple_of(lax.rem(m, PARTS) * ROWS, ROWS), ROWS)]
@@ -177,10 +200,9 @@
         pl.when(whole_slot)(go)
 
     def own(m):
-        @pl.when(lax.rem(m, PARTS) == 0)
+        @pl.when(lax.rem(m, 2 * PARTS) == 0)
         def _():
-            kv_three(m // PARTS).wait_recv()
-            kv_local_wait(m // PARTS)
+            kv_three(m // (2 * PARTS)).wait_recv()
 
     def event(m, entry):
         if len(entry) > 2:
@@ -211,14 +233,17 @@
                             if entry[0] == lag:
                                 event(m, entry)
 
-    def send_kv(h, _):
+    loads[0].wait()
+    loads[1].wait()
+    for head in range(HK):
+        stage[head, 0] = k_all[:, head * DH:(head + 1) * DH]
+        stage[head, 1] = v_all[:, head * DH:(head + 1) * DH]
+    for h in range(HLOC):
+        for o in (2, 1, 3):
+            kv_copy(o, h).start()
         for i in range(2):
-            for o in (2, 1, 3):
-                kv_copy(o, h, i).start()
-            kv_local(h, i).start()
-        return 0
-
-    lax.fori_loop(0, HLOC, send_kv, 0)
+            kv[2 * h + i, 0, own_rows] = stage[y * HLOC + h, i]
+    loads[2].wait()
 
     def whole(g, slots=6):
         ref = kv.at[g, pl.ds(0, slots)]
@@ -258,6 +283,9 @@
             start = op(start, rows[i:i + 8])
         return start
 
+    def order(j):
+        return lax.rem(2 + 3 * j + 3 * (j // 2) + 2 * (j // 3), NHEAD)
+
     def weigh(h, j):
         @pl.when(j == 0)
         def _():
@@ -266,7 +294,7 @@
             q_local_wait(h)
             collect(2 * h)
 
-        c = lax.rem(y + j + 1, NHEAD)
+        c = lax.rem(y + order(j), NHEAD)
         for g in range(GRP):
             turned[:, g * TOK:(g + 1) * TOK] = qbuf[h, c, :, g * DH:(g + 1) * DH].T
         valid, _ = picks(h)
@@ -304,7 +332,7 @@
             for t in range(TOPK + 1):
                 flipped[:, t * BLK:(t + 1) * BLK] = blocks[1, t].T
 
-        o = lax.rem(j + 1, NHEAD)
+        o = order(j)
         c = lax.rem(y + o, NHEAD)
         for side in range(2):
             q0 = side * 2 * TOK
@@ -312,8 +340,14 @@
             res = acc / totals[c, 0:1, q0:q0 + 2 * TOK]
             for g in range(2):
                 obuf[h, c, :, q0 + g * DH:q0 + (g + 1) * DH] = res[:, g * TOK:(g + 1) * TOK].T.astype(jnp.bfloat16)
-        for k in (1, 2, 3):
+        for k in (1, 3):
             pl.when(o == k)(lambda: out_copy(k, h).start())
+
+        @pl.when(o == 2)
+        def _():
+            for k in range(2):
+                out_via(h, k).start()
+
         pl.when(o == 0)(lambda: out_local(h).start())
 
     def before(n):
@@ -323,11 +357,13 @@
         h, kind, j = k // 8, lax.rem(k // 4, 2), lax.rem(k, 4)
         pl.when(kind == 0)(lambda: weigh(h, j))
         pl.when(kind == 1)(lambda: attend(h, j))
+        pl.when((k == 9) | (k == 14))(lambda: out_pass(k // 14))
         return 0
 
     def tick(n, _):
         step(n)
-        pl.when((n == 3) | (n == 6))(lambda: send_q(n // 6))
+        pl.when((n == 1) | (n == 2))(lambda: send_q(n // 2))
+        pl.when((n == 4) | (n == 6))(lambda: q_pass(n // 6))
         lax.fori_loop(before(n), before(n + 1), item, 0)
         return 0
 
@@ -349,7 +385,6 @@
                     remote(ref, ref, win_send.at[g], sib_recv.at[g], right).wait_send()
 
     def finish(g, _):
-        kv_three(g).wait_send()
         whole(g).wait_send()
         pl.when(g < GROUPS - 1)(lambda: sent(g, 0))
         pl.when(g == GROUPS - 1)(lambda: sent(g, PIECES - 1))
@@ -357,6 +392,9 @@
 
     lax.fori_loop(0, GROUPS, finish, 0)
     for h in range(HLOC):
+        kv_three(h).wait_send()
+        three(q_relay.at[h], q_relay_send.at[h], q_recv.at[h]).wait_send()
+        three(out_relay_buf.at[h], relay_send.at[h], out_recv.at[h]).wait_send()
         q_three(h).wait_send()
         out_three(h).wait()
         out_local(h).wait()
@@ -385,11 +423,19 @@
             pltpu.VMEM((NHEAD, 8, GRP * TOK), jnp.float32),
             pltpu.VMEM((DH, (TOPK + 1) * BLK), jnp.bfloat16),
             pltpu.VMEM((DH, GRP * TOK), jnp.bfloat16),
-            dma((GROUPS,)), dma((GROUPS,)),
+            pltpu.VMEM((TOK, HK * DH), jnp.bfloat16),
+            pltpu.VMEM((TOK, HK * DH), jnp.bfloat16),
+            pltpu.VMEM((TOK, HQ * DH), jnp.bfloat16),
+            pltpu.VMEM((HK, 2, TOK, DH), jnp.bfloat16),
+            pltpu.VMEM((HLOC, 2, TOK // 2, WIDE), jnp.bfloat16),
+            pltpu.VMEM((HLOC, 2, TOK // 2, WIDE), jnp.bfloat16),
+            dma((HLOC,)), dma((HLOC,)),
             dma((HLOC,)), dma((HLOC,)),
             dma((GROUPS,)), dma((PIECES, 6)),
             dma((GROUPS,)), dma((GROUPS,)),
             dma((HLOC,)), dma((HLOC,)),
+            dma((HLOC, 2)), dma((HLOC,)),
+            dma((HLOC, 2)), dma((HLOC,)),
             dma((GROUPS + 2 * HLOC,)),
         ],
         compiler_params=pltpu.CompilerParams(

time: 66.2 us -> 68.4 us (1.033)
  Pallas kernels: 64.6 us -> 67 us
    pallas_call x1, Pallas kernels: 64.6 us -> 67 us  [on_device(): pl.pallas_call(body, out_shape=pltpu.VMEM(query.shape, jnp.bfloat16), in_...]
where the time goes in v8:
time: 68.4 us; the launch traced here: 68 us
  Pallas kernels  67 us (98%)
  local copies, waits for them, and re-layouts  0.97 us (1%)
    pallas_call x1, Pallas kernels, on_device(): pl.pallas_call(body, out_shape=pltpu.VMEM(query.shape, jnp.bfloat16), in_...  67 us

profile of v8, /device:TPU:160, one launch (start us, length us, event | category | flops | bytes accessed | tf_op | source)
XLA Modules:
  0.0 68.0 jit_solution(2811986637144009280)
XLA Ops:
  0.0 67.0 %window_attention.1 = bf16[128,4096]{1,0:T(8,128)(2,1)S(1)} custom-call(s32[1,2,3]{2,1,0:T(2,128)} %refs_0_.1, bf16[128,4096]{1,0:T(8,128)(2,1)} %refs_1_.1, bf16[128,1024]{1,0:T(8,128)(2,1)} %refs_2_.1, bf16[128,1024]{1,0:T(8,128)(2,1)} %refs_3_.1), custom_call_target="tpu_custom_call" | custom-call | flops 4294967296 | bytes 4194304 | tf_op jit(solution)/shard_map/window_attention/pallas_call | solution.py:411
  67.0 1.0 %copy.6 = bf16[128,4096]{1,0:T(8,128)(2,1)} copy(bf16[128,4096]{1,0:T(8,128)(2,1)S(1)} %window_attention.1) | data formatting | bytes 2097152

commit v9 on v7

--- a/solution.py
+++ b/solution.py
@@ -55,6 +55,7 @@
 
 
 def kernel(nseq, chosen, query, keys, values, out, kv, blocks, qbuf, obuf, scores, weights, totals, flipped, turned,
+           give, got, mine, theirs, asked, ask_send, ask_recv,
            own_send, own_recv, q_send, q_recv, win_send, win_recv, sib_send, sib_recv,
            out_send, out_recv, local_sem):
     nz = nseq // (2 * NX)
@@ -162,19 +163,6 @@
 
     def arrived(m, r):
         remote(piece(m, 2 * r), piece(m, 2 * r), win_send.at[m // PARTS], win_recv.at[m, r - 1], up).wait_recv()
-
-    def share(m, r):
-        g = m // PARTS
-
-        def go():
-            remote(kv.at[g, 2 * r], kv.at[g, 2 * r + 1 - 2 * core], sib_send.at[g], sib_recv.at[g], sibling).start()
-
-        whole_slot = lax.rem(m, PARTS) == PARTS - 1
-        if r == 0:
-            whole_slot = whole_slot & (core == 0)
-        elif r == 6:
-            whole_slot = whole_slot & (core == 1)
-        pl.when(whole_slot)(go)
 
     def own(m):
         @pl.when(lax.rem(m, PARTS) == 0)
@@ -196,7 +184,6 @@
                 own(m)
             else:
                 pl.when(place >= entry[1])(lambda: arrived(m, entry[1]))
-            share(m, entry[1])
 
     def step(n):
         for xx in range(NX):
@@ -220,32 +207,63 @@
 
     lax.fori_loop(0, HLOC, send_kv, 0)
 
-    def whole(g, slots=6):
-        ref = kv.at[g, pl.ds(0, slots)]
-        return remote(ref, ref, sib_send.at[g], sib_recv.at[g], sibling)
+    row = lax.broadcasted_iota(jnp.int32, (8, DH), 0)
+    listed = jnp.zeros((8, DH), jnp.int32)
+    for h in range(HLOC):
+        for t in range(TOPK):
+            listed = jnp.where(row == h * TOPK + t, chosen[0, h, t], listed)
+    mine[...] = listed
+    ask = remote(mine, theirs, ask_send.at[0], ask_recv.at[0], sibling)
+    ask.start()
+    ask.wait()
+    read = pltpu.make_async_copy(theirs, asked, local_sem.at[GROUPS + 2 * HLOC])
+    read.start()
+    read.wait()
+
+    def exchange(g):
+        return remote(give.at[g], got.at[g], sib_send.at[g], sib_recv.at[g], sibling)
 
     def picks(h):
-        valid, slot = [None], [0]
-        for t in range(TOPK):
-            pick = chosen[0, h, t]
-            valid.append(pick >= 0)
-            slot.append(seq - pick)
-        return valid, slot
+        return [None] + [chosen[0, h, t] >= 0 for t in range(TOPK)]
+
+    def choose(g, named, rows, found):
+        for r in range(SLOTS // 2 + 1):
+            block = kv[g, 2 * r, rows]
+            for t in range(TOPK):
+                found[t] = jnp.where(named[t] == seq - 2 * r, block, found[t])
+        return found
+
+    def known(index):
+        return jnp.where(index >= 0, index, -64)
+
+    def part_rows(i):
+        return pl.ds(pl.multiple_of(i * DH, DH), DH)
+
+    def offer(g):
+        named = [known(asked[(g // 2) * TOPK + t, 0]) for t in range(TOPK)]
+
+        def part(i, _):
+            rows = part_rows(i)
+            found = choose(g, named, rows, [kv[g, 0, rows]] * TOPK)
+            for t in range(TOPK):
+                give[g, t, rows] = found[t]
+            return 0
+
+        lax.fori_loop(0, BLK // DH, part, 0)
+        exchange(g).start()
 
     def collect(g):
-        _, slot = picks(g // 2)
+        exchange(g).wait_recv()
+        named = [known(chosen[0, g // 2, t]) for t in range(TOPK)]
+        away = [(chosen[0, g // 2, t] >= 0) & (lax.rem(seq - named[t], 2) == 1) for t in range(TOPK)]
 
         def part(i, _):
-            rows = pl.ds(pl.multiple_of(i * DH, DH), DH)
+            rows = part_rows(i)
             block = kv[g, 0, rows]
             blocks[g % 2, 0, rows] = block
-            found = [block] * TOPK
-            for d in range(1, SLOTS):
-                block = kv[g, d, rows]
-                for t in range(TOPK):
-                    found[t] = jnp.where(slot[t + 1] == d, block, found[t])
+            found = choose(g, named, rows, [block] * TOPK)
             for t in range(TOPK):
-                blocks[g % 2, t + 1, rows] = found[t]
+                blocks[g % 2, t + 1, rows] = jnp.where(away[t], got[g, t, rows], found[t])
             return 0
 
         lax.fori_loop(0, BLK // DH, part, 0)
@@ -261,7 +279,6 @@
     def weigh(h, j):
         @pl.when(j == 0)
         def _():
-            whole(2 * h).wait_recv()
             q_three(h).wait_recv()
             q_local_wait(h)
             collect(2 * h)
@@ -269,7 +286,7 @@
         c = lax.rem(y + j + 1, NHEAD)
         for g in range(GRP):
             turned[:, g * TOK:(g + 1) * TOK] = qbuf[h, c, :, g * DH:(g + 1) * DH].T
-        valid, _ = picks(h)
+        valid = picks(h)
         top = None
         for t in range(TOPK + 1):
             high = jnp.full((8, GRP * TOK), NEG, jnp.float32)
@@ -299,7 +316,6 @@
     def attend(h, j):
         @pl.when(j == 0)
         def _():
-            whole(2 * h + 1).wait_recv()
             collect(2 * h + 1)
             for t in range(TOPK + 1):
                 flipped[:, t * BLK:(t + 1) * BLK] = blocks[1, t].T
@@ -327,6 +343,8 @@
 
     def tick(n, _):
         step(n)
+        last = n - (10 - 2 * x + x // 3)
+        pl.when((last >= 0) & (last < PIECES) & (lax.rem(last, PARTS) == PARTS - 1))(lambda: offer(last // PARTS))
         pl.when((n == 3) | (n == 6))(lambda: send_q(n // 6))
         lax.fori_loop(before(n), before(n + 1), item, 0)
         return 0
@@ -350,7 +368,7 @@
 
     def finish(g, _):
         kv_three(g).wait_send()
-        whole(g).wait_send()
+        exchange(g).wait_send()
         pl.when(g < GROUPS - 1)(lambda: sent(g, 0))
         pl.when(g == GROUPS - 1)(lambda: sent(g, PIECES - 1))
         return 0
@@ -385,12 +403,18 @@
             pltpu.VMEM((NHEAD, 8, GRP * TOK), jnp.float32),
             pltpu.VMEM((DH, (TOPK + 1) * BLK), jnp.bfloat16),
             pltpu.VMEM((DH, GRP * TOK), jnp.bfloat16),
+            pltpu.VMEM((GROUPS, TOPK, BLK, DH), jnp.bfloat16),
+            pltpu.VMEM((GROUPS, TOPK, BLK, DH), jnp.bfloat16),
+            pltpu.VMEM((8, DH), jnp.int32),
+            pltpu.VMEM((8, DH), jnp.int32),
+            pltpu.SMEM((8, DH), jnp.int32),
+            dma((1,)), dma((1,)),
             dma((GROUPS,)), dma((GROUPS,)),
             dma((HLOC,)), dma((HLOC,)),
             dma((GROUPS,)), dma((PIECES, 6)),
             dma((GROUPS,)), dma((GROUPS,)),
             dma((HLOC,)), dma((HLOC,)),
-            dma((GROUPS + 2 * HLOC,)),
+            dma((GROUPS + 2 * HLOC + 1,)),
         ],
         compiler_params=pltpu.CompilerParams(
             collective_id=0, has_side_effects=True, vmem_limit_bytes=56 * 1024 * 1024),

time: 66.2 us -> 67 us (1.012)
  Pallas kernels: 64.6 us -> 65.7 us
    pallas_call x1, Pallas kernels: 64.6 us -> 65.7 us  [on_device(): pl.pallas_call(body, out_shape=pltpu.VMEM(query.shape, jnp.bfloat16), in_...]
where the time goes in v9:
time: 67 us; the launch traced here: 66.7 us
  Pallas kernels  65.7 us (98%)
  local copies, waits for them, and re-layouts  0.97 us (1%)
    pallas_call x1, Pallas kernels, on_device(): pl.pallas_call(body, out_shape=pltpu.VMEM(query.shape, jnp.bfloat16), in_...  65.7 us

profile of v9, /device:TPU:160, one launch (start us, length us, event | category | flops | bytes accessed | tf_op | source)
XLA Modules:
  0.0 66.7 jit_solution(12562047650719957217)
XLA Ops:
  0.0 65.7 %window_attention.1 = bf16[128,4096]{1,0:T(8,128)(2,1)S(1)} custom-call(s32[1,2,3]{2,1,0:T(2,128)} %refs_0_.1, bf16[128,4096]{1,0:T(8,128)(2,1)} %refs_1_.1, bf16[128,1024]{1,0:T(8,128)(2,1)} %refs_2_.1, bf16[128,1024]{1,0:T(8,128)(2,1)} %refs_3_.1), custom_call_target="tpu_custom_call" | custom-call | flops 4294967296 | bytes 4194304 | tf_op jit(solution)/shard_map/window_attention/pallas_call | solution.py:391
  65.7 1.0 %copy.6 = bf16[128,4096]{1,0:T(8,128)(2,1)} copy(bf16[128,4096]{1,0:T(8,128)(2,1)S(1)} %window_attention.1) | data formatting | bytes 2097152

commit v10 on v7

--- a/solution.py
+++ b/solution.py
@@ -25,19 +25,19 @@
 WIDE = GRP * DH
 STRIP = 32
 NEG = -1e30
-RATE = math.log2(math.e) / math.sqrt(DH)
+RATE = 1.0 / math.sqrt(DH)
 MESH = pl.DeviceIdType.MESH
 
 ROUTES = {
     0: [
         (0, 0), (0, "Z", 0, 4), (0, "P", 0, 1), (0, "M", 0, 3), (2, 4),
-        (2, "P", 4, 5), (4, 1), (4, "Z", 1, 5, 6, 8), (4, 3), (4, "M", 3, 6), (6, 2),
-        (6, "Z", 2, 6), (9, 6), (10, 5),
+        (2, "P", 4, 5), (4, 1), (4, "Z", 1, 5), (4, 3), (4, "M", 3, 6),
+        (6, 2), (6, "Z", 2, 6), (6, 5), (8, 6),
     ],
     1: [
         (0, 0), (0, "Z", 0, 4), (0, "P", 0, 1), (2, 4), (2, "M", 4, 3),
         (2, "P", 4, 5), (2, 1), (4, 3), (4, 5), (6, 2),
-        (6, "Z", 2, 6), (8, 6), (8, "M", 6, 5, 0, 6),
+        (6, "Z", 2, 6), (8, 6),
     ],
     2: [
         (0, 0), (0, "Z", 0, 4), (0, "P", 0, 1), (2, 4), (2, "M", 4, 3),
@@ -50,8 +50,8 @@
         (4, "P", 5, 2), (4, 2), (5, 6),
     ],
 }
-TICKS = 18
-ITEM_TICKS = (12, 12, 13, 14, 14, 14, 15, 16, 16, 16, 17, 17, 17, 17, 17, 17)
+TICKS = 16
+ITEM_TICKS = (10, 10, 11, 12, 12, 12, 13, 14, 14, 14, 15, 15, 15, 15, 15, 15)
 
 
 def kernel(nseq, chosen, query, keys, values, out, kv, blocks, qbuf, obuf, scores, weights, totals, flipped, turned,
@@ -187,8 +187,6 @@
             there = place >= entry[2]
             if entry[1] == "Z":
                 there = there & (z < nz - 1)
-            if len(entry) > 4:
-                there = there & (m >= entry[4]) & (m < entry[5])
             to = {"Z": up, "P": right, "M": left}[entry[1]]
             pl.when(there)(lambda: forward(m, to, entry[2], entry[3]))
         else:
@@ -289,7 +287,7 @@
 
             def band(i, total):
                 rows = pl.ds(pl.multiple_of(i * STRIP, STRIP), STRIP)
-                p = jnp.exp2((scores[t, rows] - shift) * RATE)
+                p = jnp.exp((scores[t, rows] - shift) * RATE)
                 weights[c, pl.ds(pl.multiple_of(t * BLK + i * STRIP, STRIP), STRIP)] = p.astype(jnp.bfloat16)
                 return fold(jnp.add, total, p)
 
@@ -333,13 +331,13 @@
 
     lax.fori_loop(0, TICKS, tick, 0)
 
-    def sent(g, m):
+    def sent(g):
         for xx in range(NX):
             for low, high in ((0, 1), (1, 2), (2, nz - 1), (nz - 1, nz)):
                 count = 0
                 for entry in ROUTES[xx]:
                     if len(entry) > 2 and low * NX + xx >= entry[2] and (entry[1] != "Z" or low < nz - 1):
-                        count += len(entry) == 4 or entry[4] <= m < entry[5]
+                        count += 1
                 if count == 0:
                     continue
 
@@ -351,8 +349,7 @@
     def finish(g, _):
         kv_three(g).wait_send()
         whole(g).wait_send()
-        pl.when(g < GROUPS - 1)(lambda: sent(g, 0))
-        pl.when(g == GROUPS - 1)(lambda: sent(g, PIECES - 1))
+        sent(g)
         return 0
 
     lax.fori_loop(0, GROUPS, finish, 0)

time: 66.2 us -> 63.7 us (0.962)
  Pallas kernels: 64.6 us -> 61.9 us
    pallas_call x1, Pallas kernels: 64.6 us -> 61.9 us  [on_device(): pl.pallas_call(body, out_shape=pltpu.VMEM(query.shape, jnp.bfloat16), in_...]
where the time goes in v10:
time: 63.7 us; the launch traced here: 62.9 us
  Pallas kernels  61.9 us (97%)
  local copies, waits for them, and re-layouts  0.97 us (2%)
    pallas_call x1, Pallas kernels, on_device(): pl.pallas_call(body, out_shape=pltpu.VMEM(query.shape, jnp.bfloat16), in_...  61.9 us

profile of v10, /device:TPU:160, one launch (start us, length us, event | category | flops | bytes accessed | tf_op | source)
XLA Modules:
  0.0 62.9 jit_solution(457344005759968781)
XLA Ops:
  0.0 61.9 %window_attention.1 = bf16[128,4096]{1,0:T(8,128)(2,1)S(1)} custom-call(s32[1,2,3]{2,1,0:T(2,128)} %refs_0_.1, bf16[128,4096]{1,0:T(8,128)(2,1)} %refs_1_.1, bf16[128,1024]{1,0:T(8,128)(2,1)} %refs_2_.1, bf16[128,1024]{1,0:T(8,128)(2,1)} %refs_3_.1), custom_call_target="tpu_custom_call" | custom-call | flops 4294967296 | bytes 4194304 | tf_op jit(solution)/shard_map/window_attention/pallas_call | solution.py:370
  61.9 1.0 %copy.6 = bf16[128,4096]{1,0:T(8,128)(2,1)} copy(bf16[128,4096]{1,0:T(8,128)(2,1)S(1)} %window_attention.1) | data formatting | bytes 2097152

commit v11 on v10

--- a/solution.py
+++ b/solution.py
@@ -51,12 +51,12 @@
     ],
 }
 TICKS = 16
-ITEM_TICKS = (10, 10, 11, 12, 12, 12, 13, 14, 14, 14, 15, 15, 15, 15, 15, 15)
-
-
-def kernel(nseq, chosen, query, keys, values, out, kv, blocks, qbuf, obuf, scores, weights, totals, flipped, turned,
+ITEM_TICKS = (9, 10, 10, 11, 11, 12, 12, 12, 13, 13, 14, 15, 15, 15, 15, 15)
+
+
+def kernel(nseq, chosen, query, keys, values, out, kv, blocks, qbuf, obuf, scores, weights, totals, flipped, turned, relay,
            own_send, own_recv, q_send, q_recv, win_send, win_recv, sib_send, sib_recv,
-           out_send, out_recv, local_sem):
+           out_send, out_recv, relay_recv, relay_send, local_sem):
     nz = nseq // (2 * NX)
     seq = lax.axis_index("seq")
     y = lax.axis_index("head")
@@ -152,6 +152,20 @@
         for o in (2, 1, 3):
             q_copy(o, h).start()
         q_local(h).start()
+
+    def half(k):
+        return pl.ds(k * TOK // 2, TOK // 2)
+
+    def out_via(h, k):
+        return remote(obuf.at[h, partner(2)[1], half(k)], relay.at[h, k], out_send.at[h], relay_recv.at[h, k],
+                      partner(1 + 2 * k))
+
+    def out_pass(h):
+        for k in range(2):
+            ref = relay.at[h, k]
+            remote(ref, ref, out_send.at[h], relay_recv.at[h, k], sibling).wait_recv()
+            remote(ref, out_place(partner(3 - 2 * k)[1], h).at[half(k)], relay_send.at[h], out_recv.at[h],
+                   partner(1 + 2 * k)).start()
 
     def piece(m, slot):
         return kv.at[m // PARTS, slot, pl.ds(pl.multiple_of(lax.rem(m, PARTS) * ROWS, ROWS), ROWS)]
@@ -256,6 +270,9 @@
             start = op(start, rows[i:i + 8])
         return start
 
+    def order(j):
+        return lax.rem(2 + 3 * j + 3 * (j // 2) + 2 * (j // 3), NHEAD)
+
     def weigh(h, j):
         @pl.when(j == 0)
         def _():
@@ -264,7 +281,7 @@
             q_local_wait(h)
             collect(2 * h)
 
-        c = lax.rem(y + j + 1, NHEAD)
+        c = lax.rem(y + order(j), NHEAD)
         for g in range(GRP):
             turned[:, g * TOK:(g + 1) * TOK] = qbuf[h, c, :, g * DH:(g + 1) * DH].T
         valid, _ = picks(h)
@@ -302,7 +319,7 @@
             for t in range(TOPK + 1):
                 flipped[:, t * BLK:(t + 1) * BLK] = blocks[1, t].T
 
-        o = lax.rem(j + 1, NHEAD)
+        o = order(j)
         c = lax.rem(y + o, NHEAD)
         for side in range(2):
             q0 = side * 2 * TOK
@@ -310,8 +327,14 @@
             res = acc / totals[c, 0:1, q0:q0 + 2 * TOK]
             for g in range(2):
                 obuf[h, c, :, q0 + g * DH:q0 + (g + 1) * DH] = res[:, g * TOK:(g + 1) * TOK].T.astype(jnp.bfloat16)
-        for k in (1, 2, 3):
+        for k in (1, 3):
             pl.when(o == k)(lambda: out_copy(k, h).start())
+
+        @pl.when(o == 2)
+        def _():
+            for k in range(2):
+                out_via(h, k).start()
+
         pl.when(o == 0)(lambda: out_local(h).start())
 
     def before(n):
@@ -321,6 +344,7 @@
         h, kind, j = k // 8, lax.rem(k // 4, 2), lax.rem(k, 4)
         pl.when(kind == 0)(lambda: weigh(h, j))
         pl.when(kind == 1)(lambda: attend(h, j))
+        pl.when((k == 9) | (k == 15))(lambda: out_pass(k // 15))
         return 0
 
     def tick(n, _):
@@ -356,6 +380,7 @@
     for h in range(HLOC):
         q_three(h).wait_send()
         out_three(h).wait()
+        three(relay.at[h], relay_send.at[h], out_recv.at[h]).wait_send()
         out_local(h).wait()
 
 
@@ -382,11 +407,13 @@
             pltpu.VMEM((NHEAD, 8, GRP * TOK), jnp.float32),
             pltpu.VMEM((DH, (TOPK + 1) * BLK), jnp.bfloat16),
             pltpu.VMEM((DH, GRP * TOK), jnp.bfloat16),
+            pltpu.VMEM((HLOC, 2, TOK // 2, WIDE), jnp.bfloat16),
             dma((GROUPS,)), dma((GROUPS,)),
             dma((HLOC,)), dma((HLOC,)),
             dma((GROUPS,)), dma((PIECES, 6)),
             dma((GROUPS,)), dma((GROUPS,)),
             dma((HLOC,)), dma((HLOC,)),
+            dma((HLOC, 2)), dma((HLOC,)),
             dma((GROUPS + 2 * HLOC,)),
         ],
         compiler_params=pltpu.CompilerParams(

time: 63.7 us -> 62.8 us (0.986); the launches traced: 62.9 us -> 62.7 us
  no operation moved by 1% of the time
where the time goes in v11:
time: 62.8 us; the launch traced here: 62.7 us
  Pallas kernels  61.7 us (98%)
  local copies, waits for them, and re-layouts  0.97 us (2%)
    pallas_call x1, Pallas kernels, on_device(): pl.pallas_call(body, out_shape=pltpu.VMEM(query.shape, jnp.bfloat16), in_...  61.7 us

profile of v11, /device:TPU:160, one launch (start us, length us, event | category | flops | bytes accessed | tf_op | source)
XLA Modules:
  0.0 62.7 jit_solution(12090874104563040304)
XLA Ops:
  0.0 61.7 %window_attention.1 = bf16[128,4096]{1,0:T(8,128)(2,1)S(1)} custom-call(s32[1,2,3]{2,1,0:T(2,128)} %refs_0_.1, bf16[128,4096]{1,0:T(8,128)(2,1)} %refs_1_.1, bf16[128,1024]{1,0:T(8,128)(2,1)} %refs_2_.1, bf16[128,1024]{1,0:T(8,128)(2,1)} %refs_3_.1), custom_call_target="tpu_custom_call" | custom-call | flops 4294967296 | bytes 4194304 | tf_op jit(solution)/shard_map/window_attention/pallas_call | solution.py:395
  61.7 1.0 %copy.6 = bf16[128,4096]{1,0:T(8,128)(2,1)} copy(bf16[128,4096]{1,0:T(8,128)(2,1)S(1)} %window_attention.1) | data formatting | bytes 2097152

commit v12 on v11

--- a/solution.py
+++ b/solution.py
@@ -19,7 +19,7 @@
 NX = 4
 SLOTS = 13
 GROUPS = 2 * HLOC
-PARTS = 2
+PARTS = 1
 PIECES = GROUPS * PARTS
 ROWS = BLK // PARTS
 WIDE = GRP * DH
@@ -30,28 +30,28 @@
 
 ROUTES = {
     0: [
-        (0, 0), (0, "Z", 0, 4), (0, "P", 0, 1), (0, "M", 0, 3), (2, 4),
-        (2, "P", 4, 5), (4, 1), (4, "Z", 1, 5), (4, 3), (4, "M", 3, 6),
-        (6, 2), (6, "Z", 2, 6), (6, 5), (8, 6),
+        (0, 0), (0, "Z", 0, 4), (0, "P", 0, 1), (0, "M", 0, 3), (1, 4),
+        (1, "P", 4, 5), (2, 1), (2, "Z", 1, 5), (2, 3), (2, "M", 3, 6),
+        (3, 2), (3, "Z", 2, 6), (3, 5), (4, 6),
     ],
     1: [
-        (0, 0), (0, "Z", 0, 4), (0, "P", 0, 1), (2, 4), (2, "M", 4, 3),
-        (2, "P", 4, 5), (2, 1), (4, 3), (4, 5), (6, 2),
-        (6, "Z", 2, 6), (8, 6),
+        (0, 0), (0, "Z", 0, 4), (0, "P", 0, 1), (1, 4), (1, "M", 4, 3),
+        (1, "P", 4, 5), (1, 1), (2, 3), (2, 5), (3, 2),
+        (3, "Z", 2, 6), (4, 6),
     ],
     2: [
-        (0, 0), (0, "Z", 0, 4), (0, "P", 0, 1), (2, 4), (2, "M", 4, 3),
-        (2, 1), (2, "P", 1, 2), (4, 3), (4, "M", 3, 2), (4, 2),
-        (4, "Z", 2, 6), (4, 5), (6, 6),
+        (0, 0), (0, "Z", 0, 4), (0, "P", 0, 1), (1, 4), (1, "M", 4, 3),
+        (1, 1), (1, "P", 1, 2), (2, 3), (2, "M", 3, 2), (2, 2),
+        (2, "Z", 2, 6), (2, 5), (3, 6),
     ],
     3: [
-        (0, 0), (0, "Z", 0, 4), (2, 4), (2, "P", 4, 1), (2, "M", 4, 3),
-        (2, 3), (2, "M", 3, 2), (2, 1), (2, "Z", 1, 5), (4, 5),
-        (4, "P", 5, 2), (4, 2), (5, 6),
+        (0, 0), (0, "Z", 0, 4), (1, 4), (1, "P", 4, 1), (1, "M", 4, 3),
+        (1, 3), (1, "M", 3, 2), (1, 1), (1, "Z", 1, 5), (2, 5),
+        (2, "P", 5, 2), (2, 2), (3, 6),
     ],
 }
-TICKS = 16
-ITEM_TICKS = (9, 10, 10, 11, 11, 12, 12, 12, 13, 13, 14, 15, 15, 15, 15, 15)
+TICKS = 8
+ITEM_TICKS = (4, 4, 4, 4, 5, 5, 5, 5, 6, 6, 6, 6, 7, 7, 7, 7)
 
 
 def kernel(nseq, chosen, query, keys, values, out, kv, blocks, qbuf, obuf, scores, weights, totals, flipped, turned, relay,
@@ -349,7 +349,7 @@
 
     def tick(n, _):
         step(n)
-        pl.when((n == 3) | (n == 6))(lambda: send_q(n // 6))
+        pl.when((n == 1) | (n == 2))(lambda: send_q(n // 2))
         lax.fori_loop(before(n), before(n + 1), item, 0)
         return 0
 

time: 62.8 us -> 63.4 us (level)
  no operation moved by 1% of the time
where the time goes in v12:
time: 63.4 us; the launch traced here: 62.8 us
  Pallas kernels  61.8 us (97%)
  local copies, waits for them, and re-layouts  0.97 us (2%)
    pallas_call x1, Pallas kernels, on_device(): pl.pallas_call(body, out_shape=pltpu.VMEM(query.shape, jnp.bfloat16), in_...  61.8 us

profile of v12, /device:TPU:160, one launch (start us, length us, event | category | flops | bytes accessed | tf_op | source)
XLA Modules:
  0.0 62.8 jit_solution(17691464294618258663)
XLA Ops:
  0.0 61.8 %window_attention.1 = bf16[128,4096]{1,0:T(8,128)(2,1)S(1)} custom-call(s32[1,2,3]{2,1,0:T(2,128)} %refs_0_.1, bf16[128,4096]{1,0:T(8,128)(2,1)} %refs_1_.1, bf16[128,1024]{1,0:T(8,128)(2,1)} %refs_2_.1, bf16[128,1024]{1,0:T(8,128)(2,1)} %refs_3_.1), custom_call_target="tpu_custom_call" | custom-call | flops 4294967296 | bytes 4194304 | tf_op jit(solution)/shard_map/window_attention/pallas_call | solution.py:395
  61.8 1.0 %copy.6 = bf16[128,4096]{1,0:T(8,128)(2,1)} copy(bf16[128,4096]{1,0:T(8,128)(2,1)S(1)} %window_attention.1) | data formatting | bytes 2097152

commit v13 on v11

--- a/solution.py
+++ b/solution.py
@@ -223,14 +223,12 @@
                             if entry[0] == lag:
                                 event(m, entry)
 
-    def send_kv(h, _):
-        for i in range(2):
-            for o in (2, 1, 3):
-                kv_copy(o, h, i).start()
-            kv_local(h, i).start()
-        return 0
-
-    lax.fori_loop(0, HLOC, send_kv, 0)
+    def send_kv(h, i):
+        for o in (2, 1, 3):
+            kv_copy(o, h, i).start()
+        kv_local(h, i).start()
+
+    send_kv(0, 0)
 
     def whole(g, slots=6):
         ref = kv.at[g, pl.ds(0, slots)]
@@ -349,6 +347,9 @@
 
     def tick(n, _):
         step(n)
+        pl.when(n == 0)(lambda: send_kv(0, 1))
+        pl.when(n == 1)(lambda: send_kv(1, 0))
+        pl.when(n == 2)(lambda: send_kv(1, 1))
         pl.when((n == 3) | (n == 6))(lambda: send_q(n // 6))
         lax.fori_loop(before(n), before(n + 1), item, 0)
         return 0

time: 62.8 us -> 63.4 us (level); the launches traced: 62.7 us -> 62.5 us
  no operation moved by 1% of the time
where the time goes in v13:
time: 63.4 us; the launch traced here: 62.5 us
  Pallas kernels  61.5 us (97%)
  local copies, waits for them, and re-layouts  0.97 us (2%)
    pallas_call x1, Pallas kernels, on_device(): pl.pallas_call(body, out_shape=pltpu.VMEM(query.shape, jnp.bfloat16), in_...  61.5 us

profile of v13, /device:TPU:160, one launch (start us, length us, event | category | flops | bytes accessed | tf_op | source)
XLA Modules:
  0.0 62.5 jit_solution(7728844171596248073)
XLA Ops:
  0.0 61.5 %window_attention.1 = bf16[128,4096]{1,0:T(8,128)(2,1)S(1)} custom-call(s32[1,2,3]{2,1,0:T(2,128)} %refs_0_.1, bf16[128,4096]{1,0:T(8,128)(2,1)} %refs_1_.1, bf16[128,1024]{1,0:T(8,128)(2,1)} %refs_2_.1, bf16[128,1024]{1,0:T(8,128)(2,1)} %refs_3_.1), custom_call_target="tpu_custom_call" | custom-call | flops 4294967296 | bytes 4194304 | tf_op jit(solution)/shard_map/window_attention/pallas_call | solution.py:396
  61.5 1.0 %copy.6 = bf16[128,4096]{1,0:T(8,128)(2,1)} copy(bf16[128,4096]{1,0:T(8,128)(2,1)S(1)} %window_attention.1) | data formatting | bytes 2097152

commit v14 on v11

--- a/solution.py
+++ b/solution.py
@@ -349,7 +349,7 @@
 
     def tick(n, _):
         step(n)
-        pl.when((n == 3) | (n == 6))(lambda: send_q(n // 6))
+        pl.when((n == 1) | (n == 3))(lambda: send_q(n // 3))
         lax.fori_loop(before(n), before(n + 1), item, 0)
         return 0
 

time: 62.8 us -> 62.8 us (level)
  no operation moved by 1% of the time
where the time goes in v14:
time: 62.8 us; the launch traced here: 62.7 us
  Pallas kernels  61.7 us (98%)
  local copies, waits for them, and re-layouts  0.97 us (2%)
    pallas_call x1, Pallas kernels, on_device(): pl.pallas_call(body, out_shape=pltpu.VMEM(query.shape, jnp.bfloat16), in_...  61.7 us

profile of v14, /device:TPU:160, one launch (start us, length us, event | category | flops | bytes accessed | tf_op | source)
XLA Modules:
  0.0 62.7 jit_solution(5148367811632816926)
XLA Ops:
  0.0 61.7 %window_attention.1 = bf16[128,4096]{1,0:T(8,128)(2,1)S(1)} custom-call(s32[1,2,3]{2,1,0:T(2,128)} %refs_0_.1, bf16[128,4096]{1,0:T(8,128)(2,1)} %refs_1_.1, bf16[128,1024]{1,0:T(8,128)(2,1)} %refs_2_.1, bf16[128,1024]{1,0:T(8,128)(2,1)} %refs_3_.1), custom_call_target="tpu_custom_call" | custom-call | flops 4294967296 | bytes 4194304 | tf_op jit(solution)/shard_map/window_attention/pallas_call | solution.py:395
  61.7 1.0 %copy.6 = bf16[128,4096]{1,0:T(8,128)(2,1)} copy(bf16[128,4096]{1,0:T(8,128)(2,1)S(1)} %window_attention.1) | data formatting | bytes 2097152
